TPU v7x, 32 devices: a whole 2x2x4 slice. The times are simulated.
32 devices in a mesh: section: 2 (over y), dp: 16 (over z, x, core).
Axes of the slice: x: 2, y: 2, z: 4, core: 2. Of those that a mesh axis runs over, the one named last changes fastest.
Arguments:
- stream_in: bfloat16 [32, 1024, 767], P('dp')
- cotangent: bfloat16 [32, 1024, 767], P('dp'), may hold values from -6 to 6
- weights_first: bfloat16 [2, 768, 3072], P('section')
- down_weight: bfloat16 [3072, 768], replicated, may hold values from -0.1875 to 0.1875
- segments: int32 [32, 1024], P('dp'), may hold values from 0 to 4, as said below
Outputs:
- stream_out: bfloat16 [2, 32, 1024, 767], P('section', 'dp')
- stream_grad: bfloat16 [2, 32, 1024, 767], P('section', 'dp')
- grad_first: float32 [2, 768, 3072], P('section')
- grad_down: float32 [3072, 768], P('section')
- residual_rms: float32 [2], P('section')
- token_count: int32 [2], P('section')
Inputs may be any that keep to these rules, and one draw needn't show every extreme that they name: `segments`: each row holds documents numbered in order up to 4, the last of them present in every row, over its first 512 positions or more; the rest of the row is padding with id 0.
All inputs are finite; a program needn't handle non-finite values.
Results may differ from a plain program's by a relative error of at most 0.013.
Values may be sent and summed in bfloat16 or wider, within the bound.
No kernel may reach another device: no remote copies, remote signals or barrier semaphores. Data moves between devices by JAX's collectives and lax.ppermute only.
A program may use at most 320 MiB of HBM per device.

v0:
```python
from functools import partial

import jax
import jax.numpy as jnp
from jax import lax
from jax.sharding import PartitionSpec as P

HEADS = 12
HEAD_DIM = 64


EPSILON = 1e-06
MASKED = -1e30


def shifted(block, axis, distance):
    devices = range(lax.axis_size(axis))
    route = [(i - distance, i) for i in devices if i - distance in devices]
    return lax.ppermute(block, axis, route)


def widen(compact):
    return jnp.concatenate([compact, -jnp.sum(compact, axis=-1, keepdims=True)], axis=-1)


def widen_back(grad_full):
    return grad_full[:, :-1] - grad_full[:, -1:]


def normalize(values):
    inverse = lax.rsqrt(jnp.mean(values * values, axis=-1, keepdims=True) + EPSILON)
    return (values * inverse, inverse)


def normalize_back(normed, inverse, grad_normed):
    return inverse * (grad_normed - normed * jnp.mean(grad_normed * normed, axis=-1, keepdims=True))


def compress(branch):
    return (branch - jnp.mean(branch, axis=-1, keepdims=True))[:, :-1]


def compress_back(grad_compact):
    padded = jnp.concatenate([grad_compact, jnp.zeros_like(grad_compact[:, :1])], axis=-1)
    return padded - jnp.mean(padded, axis=-1, keepdims=True)


def square_sums(rounded, segment_row):
    compact = rounded.astype(jnp.float32)
    totals = jnp.sum(compact * compact, axis=-1) + jnp.square(jnp.sum(compact, axis=-1))
    valid = segment_row > 0
    return (jnp.sum(jnp.where(valid, totals, 0.0)), jnp.sum(valid.astype(jnp.float32)))


def inner_rows(left, right):
    return lax.dot_general(
        left, right, (((0,), (0,)), ((), ())), preferred_element_type=jnp.float32
    )


def inner_cols(left, right):
    return lax.dot_general(
        left, right, (((1,), (1,)), ((), ())), preferred_element_type=jnp.float32
    )


def split_heads(packed):
    length = packed.shape[0]
    model_width = packed.shape[1] // 3
    return [
        packed[:, member * model_width : (member + 1) * model_width].reshape(
            length, HEADS, HEAD_DIM
        )
        for member in range(3)
    ]


def allowed_block(segment_keys, offset, block):
    positions = jnp.arange(segment_keys.shape[0])
    query_pos = offset + jnp.arange(block)
    same_doc = segment_keys[offset : offset + block][:, None] == segment_keys[None, :]
    return same_doc & (positions[None, :] <= query_pos[:, None])


def attend(packed, segment_row):
    queries, key_rows, values = split_heads(packed)
    length = packed.shape[0]
    block = min(512, length)
    scale_factor = HEAD_DIM ** (-0.5)
    outputs = []
    log_parts = []
    for offset in range(0, length, block):
        reach = offset + block
        scores = (
            jnp.einsum(
                "qhd,khd->hqk",
                queries[offset:reach],
                key_rows[:reach],
                preferred_element_type=jnp.float32,
            )
            * scale_factor
        )
        scores = jnp.where(allowed_block(segment_row[:reach], offset, block)[None], scores, MASKED)
        highest = jnp.max(scores, axis=-1, keepdims=True)
        exponent = jnp.exp(scores - highest)
        denominator = jnp.sum(exponent, axis=-1, keepdims=True)
        attn_probs = (exponent / denominator).astype(jnp.bfloat16)
        outputs.append(
            jnp.einsum(
                "hqk,khd->qhd", attn_probs, values[:reach], preferred_element_type=jnp.float32
            )
        )
        log_parts.append((highest + jnp.log(denominator))[..., 0])
    mixed = jnp.concatenate(outputs, axis=0).reshape(length, HEADS * HEAD_DIM).astype(jnp.bfloat16)
    return (mixed, jnp.concatenate(log_parts, axis=1))


def attend_back(packed, segment_row, grad_mixed, log_totals):
    queries, key_rows, values = split_heads(packed)
    length = packed.shape[0]
    block = min(512, length)
    scale_factor = HEAD_DIM ** (-0.5)
    grad_heads = grad_mixed.reshape(length, HEADS, HEAD_DIM)
    grad_queries = []
    grad_keys = jnp.zeros((length, HEADS, HEAD_DIM), jnp.float32)
    grad_values = jnp.zeros((length, HEADS, HEAD_DIM), jnp.float32)
    for offset in range(0, length, block):
        reach = offset + block
        query_block = queries[offset:reach]
        grad_block = grad_heads[offset:reach]
        keys_seen = key_rows[:reach]
        scores = (
            jnp.einsum("qhd,khd->hqk", query_block, keys_seen, preferred_element_type=jnp.float32)
            * scale_factor
        )
        scores = jnp.where(allowed_block(segment_row[:reach], offset, block)[None], scores, MASKED)
        attn_probs = jnp.exp(scores - log_totals[:, offset:reach, None])
        probs_low = attn_probs.astype(jnp.bfloat16)
        grad_values = grad_values.at[:reach].add(
            jnp.einsum("hqk,qhd->khd", probs_low, grad_block, preferred_element_type=jnp.float32)
        )
        grad_probs = jnp.einsum(
            "qhd,khd->hqk", grad_block, values[:reach], preferred_element_type=jnp.float32
        )
        grad_scores = attn_probs * (
            grad_probs - jnp.sum(attn_probs * grad_probs, axis=-1, keepdims=True)
        )
        grad_low = grad_scores.astype(jnp.bfloat16)
        grad_queries.append(
            jnp.einsum("hqk,khd->qhd", grad_low, keys_seen, preferred_element_type=jnp.float32)
            * scale_factor
        )
        grad_keys = grad_keys.at[:reach].add(
            jnp.einsum("hqk,qhd->khd", grad_low, query_block, preferred_element_type=jnp.float32)
            * scale_factor
        )
    model_width = HEADS * HEAD_DIM
    pieces = [jnp.concatenate(grad_queries, axis=0), grad_keys, grad_values]
    return jnp.concatenate([piece.reshape(length, model_width) for piece in pieces], axis=1).astype(
        jnp.bfloat16
    )


def on_device(stream_in, cotangent, weights_first, down_weight, segments):
    rows_dev, length, compact_width = stream_in.shape
    model_width = compact_width + 1
    on_attention = lax.axis_index("section") == 0
    layer_weights = weights_first[0]
    qkv_weights = layer_weights[:, : 3 * model_width]
    out_weights = layer_weights[:, 3 * model_width :]
    silent = jnp.zeros((length, compact_width), jnp.bfloat16)

    def attention_forward(row_index, carried):
        (
            out_rows,
            grad_rows,
            kept_qkv,
            kept_out,
            kept_totals,
            first_sum,
            down_sum,
            square_all,
            token_all,
        ) = carried
        compact = stream_in[row_index].astype(jnp.float32)
        normed, inverse = normalize(widen(compact))
        packed = jnp.dot(
            normed.astype(jnp.bfloat16), qkv_weights, preferred_element_type=jnp.float32
        ).astype(jnp.bfloat16)
        mixed, log_totals = attend(packed, segments[row_index])
        branch = jnp.dot(mixed, out_weights, preferred_element_type=jnp.float32)
        middle = (compact + compress(branch)).astype(jnp.bfloat16)
        squares, counted = square_sums(middle, segments[row_index])
        updated = (
            out_rows.at[row_index].set(middle),
            grad_rows,
            kept_qkv.at[row_index].set(packed),
            kept_out.at[row_index].set(mixed),
            kept_totals.at[row_index].set(log_totals),
            first_sum,
            down_sum,
            square_all + squares,
            token_all + counted,
        )
        return (updated, middle)

    def attention_backward(row_index, carried, received):
        (
            out_rows,
            grad_rows,
            kept_qkv,
            kept_out,
            kept_totals,
            first_sum,
            down_sum,
            square_all,
            token_all,
        ) = carried
        grad_compact = received.astype(jnp.float32)
        grad_branch = compress_back(grad_compact).astype(jnp.bfloat16)
        grad_out_weights = inner_rows(kept_out[row_index], grad_branch)
        grad_mixed = inner_cols(grad_branch, out_weights).astype(jnp.bfloat16)
        grad_packed = attend_back(
            kept_qkv[row_index], segments[row_index], grad_mixed, kept_totals[row_index]
        )
        compact = stream_in[row_index].astype(jnp.float32)
        normed, inverse = normalize(widen(compact))
        grad_qkv_weights = inner_rows(normed.astype(jnp.bfloat16), grad_packed)
        grad_normed = inner_cols(grad_packed, qkv_weights)
        grad_input = (
            grad_compact + widen_back(normalize_back(normed, inverse, grad_normed))
        ).astype(jnp.bfloat16)
        first_sum = first_sum + jnp.concatenate([grad_qkv_weights, grad_out_weights], axis=1)
        return (
            out_rows,
            grad_rows.at[row_index].set(grad_input),
            kept_qkv,
            kept_out,
            kept_totals,
            first_sum,
            down_sum,
            square_all,
            token_all,
        )

    def feed_forward(row_index, carried, received):
        (
            out_rows,
            grad_rows,
            kept_qkv,
            kept_out,
            kept_totals,
            first_sum,
            down_sum,
            square_all,
            token_all,
        ) = carried
        compact = received.astype(jnp.float32)
        normed, inverse = normalize(widen(compact))
        normed_low = normed.astype(jnp.bfloat16)
        hidden = jnp.dot(normed_low, layer_weights, preferred_element_type=jnp.float32)
        activated, gelu_pull = jax.vjp(partial(jax.nn.gelu, approximate=True), hidden)
        activated_low = activated.astype(jnp.bfloat16)
        output = (
            compact
            + compress(jnp.dot(activated_low, down_weight, preferred_element_type=jnp.float32))
        ).astype(jnp.bfloat16)
        squares, counted = square_sums(output, segments[row_index])
        grad_compact = cotangent[row_index].astype(jnp.float32)
        grad_branch = compress_back(grad_compact).astype(jnp.bfloat16)
        grad_lower = inner_rows(activated_low, grad_branch)
        grad_hidden = gelu_pull(inner_cols(grad_branch, down_weight))[0].astype(jnp.bfloat16)
        grad_upper = inner_rows(normed_low, grad_hidden)
        grad_normed = inner_cols(grad_hidden, layer_weights)
        grad_middle = (
            grad_compact + widen_back(normalize_back(normed, inverse, grad_normed))
        ).astype(jnp.bfloat16)
        updated = (
            out_rows.at[row_index].set(output),
            grad_rows.at[row_index].set(grad_middle),
            kept_qkv,
            kept_out,
            kept_totals,
            first_sum + grad_upper,
            down_sum + grad_lower,
            square_all + squares,
            token_all + counted,
        )
        return (updated, grad_middle)

    def run_step(forward_row, backward_row, mlp_row, carried, received):

        def attention_side(carried_in, received_in):
            sending = silent
            if forward_row is not None:
                carried_in, sending = attention_forward(forward_row, carried_in)
            if backward_row is not None:
                carried_in = attention_backward(backward_row, carried_in, received_in)
            return (carried_in, sending)

        def mlp_side(carried_in, received_in):
            if mlp_row is None:
                return (carried_in, silent)
            return feed_forward(mlp_row, carried_in, received_in)

        return lax.cond(on_attention, attention_side, mlp_side, carried, received)

    carried = (
        jnp.zeros((rows_dev, length, compact_width), jnp.bfloat16),
        jnp.zeros((rows_dev, length, compact_width), jnp.bfloat16),
        jnp.zeros((rows_dev, length, 3 * model_width), jnp.bfloat16),
        jnp.zeros((rows_dev, length, model_width), jnp.bfloat16),
        jnp.zeros((rows_dev, HEADS, length), jnp.float32),
        jnp.zeros((model_width, 4 * model_width), jnp.float32),
        jnp.zeros((down_weight.shape[0], model_width), jnp.float32),
        jnp.zeros((), jnp.float32),
        jnp.zeros((), jnp.float32),
    )
    received = silent
    for row_index in range(rows_dev):
        carried, sending = run_step(row_index, None, None, carried, received)
        received = shifted(sending, "section", 1)
        carried, sending = run_step(None, None, row_index, carried, received)
        received = shifted(sending, "section", -1)
        carried, sending = run_step(None, row_index, None, carried, received)
    out_rows = carried[0]
    grad_rows = carried[1]
    first_sum = carried[5]
    down_sum = carried[6]
    half_rows = down_sum.shape[0] // 2
    first_total, down_whole, square_total, token_total = lax.psum(
        (first_sum, down_sum, carried[7], carried[8]), "dp"
    )
    handed = shifted(down_whole[:half_rows].astype(jnp.bfloat16), "section", -1).astype(jnp.float32)
    down_total = jnp.where(on_attention, handed, down_whole[half_rows:])
    residual_rms = jnp.sqrt(square_total / (token_total * model_width)).reshape(1)
    slots = jnp.float32(rows_dev * length * lax.axis_size("dp"))
    counted_all = jnp.where(on_attention, token_total, slots - token_total)
    token_count = counted_all.astype(jnp.int32).reshape(1)
    return (
        out_rows[None],
        grad_rows[None],
        first_total[None],
        down_total,
        residual_rms,
        token_count,
    )


def solution(mesh):
    placed = (
        P("dp", None, None),
        P("dp", None, None),
        P("section", None, None),
        P(),
        P("dp", None),
    )
    return jax.shard_map(
        on_device,
        mesh=mesh,
        in_specs=placed,
        out_specs=(
            P("section", "dp", None, None),
            P("section", "dp", None, None),
            P("section", None, None),
            P("section", None),
            P("section"),
            P("section"),
        ),
        check_vma=False,
    )
```

profile of v0, /device:TPU:0, one launch (start us, length us, event | category | flops | bytes accessed | tf_op | source)
XLA Modules:
  0.0 1076.2 jit_solution(10388566589526814831)
XLA Ops:
  9.6 4.2 slice.822
  13.7 98.0 %conditional.6 = (bf16[2,1024,767]{1,2,0:T(8,128)(2,1)}, bf16[2,1024,2304]{2,1,0:T(8,128)(2,1)S(1)}, bf16[2,1024,768]{1,2,0:T(8,128)(2,1)S(1)}, f32[2,12,1024]{2...) conditional(s32[]{:T(128)} %convert_element_type.231, () %tuple.159, ...), branch_computations={%region_0.0_spmd, %region_1.13_spmd} | conditional | flops 7383019008 | bytes 396540320 | solution.py:306
  20.5 4.4 convolution_convert_fusion
  37.3 3.8 fusion.165
  46.3 6.7 scatter.29
  52.9 3.4 fusion.3
  59.0 5.6 fusion.11
  64.6 10.8 %fusion = (f32[12,512]{1,0:T(8,128)S(1)}, f32[12,512,1024]{2,1,0:T(8,128)}) fusion(pred[512,1024]{1,0:T(8,128)(4,1)S(1)} %copy-done.44, bf16[512,12,64]{0,2,1:T(8,128)(2,1)S(1)} %bitcast.289, bf16[1024,12,64]{0,2,1:T(8,128)(2,1)S(1)} %bitcast.286), kind=kOutput, calls=%fused_computation.3 | convolution fusion | flops 824174592 | bytes 28073984 | tf_op jit(solution)/shard_map/cond/branch_1_fun/qhd,khd->hqk/dot_general | solution.py:95
  75.4 12.3 %fusion.1 = f32[12,512]{1,0:T(8,128)S(1)} fusion(f32[12,512,1024]{2,1,0:T(8,128)} %get-tuple-element.776, f32[12,512]{1,0:T(8,128)S(1)} %get-tuple-element.775, pred[512,1024]{1,0:T(8,128)(4,1)S(1)} %copy-done.45), kind=kLoop, calls=%fused_computation.4 | loop fusion | flops 25159680 | bytes 25739264 | tf_op jit(solution)/shard_map/cond/branch_1_fun/reduce_sum | solution.py:106
  90.8 9.6 fusion.12
  106.3 3.5 scatter.28
  113.1 34.7 %collective-permute-done = bf16[1024,767]{0,1:T(8,128)(2,1)S(1)} collective-permute-done((bf16[1024,767]{0,1:T(8,128)(2,1)}, bf16[1024,767]{0,1:T(8,128)(2,1)S(1)}, u32[]{:S(2)}, u32[]{:S(2)}) %collective-permute-start) | collective-permute-done | bytes 1570848 | tf_op jit(solution)/shard_map/ppermute | solution.py:19
  147.9 16.5 %conditional.7 = (bf16[2,1024,767]{1,2,0:T(8,128)(2,1)}, bf16[2,1024,767]{1,2,0:T(8,128)(2,1)}, f32[768,3072]{1,0:T(8,128)}, f32[3072,768]{1,0:T(8,128)S(1)}, f3...) conditional(s32[]{:T(128)} %convert_element_type.231, (bf16[1024,767]{0,1:T(8,128)(2,1)S(1)}, ...), branch_computations={%region_13.23_spmd, %region_23.24_spmd} | conditional | flops 29142013952 | bytes 309809504 | solution.py:306
  159.5 4.9 broadcast_in_dim.166
  167.9 105.8 %conditional.8 = (bf16[2,1024,767]{1,2,0:T(8,128)(2,1)}, bf16[2,1024,2304]{2,1,0:T(8,128)(2,1)}, bf16[2,1024,768]{1,2,0:T(8,128)(2,1)}, f32[2,12,1024]{2,1,0:T(8...) conditional(s32[]{:T(128)} %convert_element_type.231, (bf16[2,1024,767]{1,2,0:T(8,128)(2,1)}, ...), branch_computations={%region_24.25_spmd, %region_25.37_spmd} | conditional | flops 7383019008 | bytes 415064608 | solution.py:306
  178.8 7.9 copy.94
  186.7 9.0 bitcast_dynamic-update-slice_fusion
  213.9 3.4 fusion.22
  219.9 5.6 fusion.30
  225.6 10.6 fusion.19
  236.2 12.3 %fusion.20 = f32[12,512]{1,0:T(8,128)S(1)} fusion(f32[12,512,1024]{2,1,0:T(8,128)} %get-tuple-element.792, f32[12,512]{1,0:T(8,128)S(1)} %get-tuple-element.791, pred[512,1024]{1,0:T(8,128)(4,1)S(1)} %copy-done.43), kind=kLoop, calls=%fused_computation.50 | loop fusion | flops 25159680 | bytes 25739264 | tf_op jit(solution)/shard_map/cond/branch_1_fun/reduce_sum | solution.py:106
  251.6 9.9 fusion.31
  276.2 162.8 %conditional.9 = ((bf16[2,1024,767]{1,2,0:T(8,128)(2,1)}, f32[768,3072]{1,0:T(8,128)})) conditional(s32[]{:T(128)} %convert_element_type.231, (bf16[2,1024,767]{1,2,0:T(8,128)(2,1)}, f32[768,3072]{1,0:T(8,128)}) %tuple.165, (bf16[1024,767]{0,1:T(8,128)(2,1)}, bf16[2,1024,767]{1,0,2:T(2,128)(2,1)}, s32[2,1024]{1,0:T(2,128)S(1)}, ...), branch_computations={%region_37.38_spmd, %region_38.45_spmd} | conditional | flops 15912252416 | bytes 623048960 | solution.py:306
  290.5 5.2 convolution_bitcast_fusion
  295.7 12.7 %copy.71 = bf16[2,1024,2304]{1,2,0:T(8,128)(2,1)} copy(bf16[2,1024,2304]{2,1,0:T(8,128)(2,1)} %get-tuple-element.668) | data formatting | bytes 18874368 | tf_op jit(solution)/shard_map
  315.0 4.0 fusion.59
  319.0 6.8 multiply_reduce_fusion.3
  325.8 7.0 multiply_convert_fusion.5
  337.1 10.3 fusion.175
  347.4 12.8 %fusion.49 = bf16[1024,12,64]{0,2,1:T(8,128)(2,1)} fusion(f32[512,12,64]{0,2,1:T(8,128)S(1)} %copy-done.70, bf16[512,12,64]{0,2,1:T(8,128)(2,1)S(1)} %bitcast.300, f32[12,512,1024]{2,1,0:T(8,128)} %fusion.175, f32[12,512]{1,0:T(8,128)S(1)} %get-tuple-element.739, pred[512,1024]{1,0:T(8,128)(4,1)S(1)} %copy-done.40), kind=kOutput, calls=%fused_computation.118 | convolution fusion | flops 832045056 | bytes 29646848 | tf_op jit(solution)/shard_map/cond/branch_1_fun/hqk,qhd->khd/dot_general | solution.py:140
  360.2 18.2 %multiply_reduce_fusion.2 = (f32[12,512]{1,0:T(8,128)S(1)}, f32[12,512,1024]{2,1,0:T(8,128)}) fusion(f32[12,512,1024]{2,1,0:T(8,128)} %fusion.175, f32[12,512]{1,0:T(8,128)S(1)} %get-tuple-element.739, pred[512,1024]{1,0:T(8,128)(4,1)} %fusion.51, bf16[512,12,64]{0,2,1:T(8,128)(2,1)} %bitcast.299, bf16[1024,12,64]{0,2,1:T(8,128)(2,1)} %bitcast.279), kind=kOutput, calls=%fused_computation.97 | convolution fusion | flops 836757504 | bytes 53264384 | tf_op jit(solution)/shard_map/cond/branch_1_fun/qhd,khd->hqk/dot_general | solution.py:142
  378.4 17.7 %multiply_convert_fusion.4 = bf16[12,512,1024]{2,1,0:T(8,128)(2,1)S(1)} fusion(f32[12,512,1024]{2,1,0:T(8,128)} %get-tuple-element.746, f32[12,512,1024]{2,1,0:T(8,128)} %fusion.175, f32[12,512]{1,0:T(8,128)S(1)} %get-tuple-element.745, f32[12,512]{1,0:T(8,128)S(1)} %get-tuple-element.739, pred[512,1024]{1,0:T(8,128)(4,1)} %fusion.51), kind=kLoop, calls=%fused_computation.96 | loop fusion | flops 37748736 | bytes 63488000 | tf_op jit(solution)/shard_map/cond/branch_1_fun/convert_element_type | solution.py:148
  396.1 4.6 copy-done.3
  400.7 3.6 fusion.50
  404.2 8.5 fusion.62
  414.6 6.6 multiply_reduce_fusion.4
  423.1 3.9 fusion.52
  427.0 8.7 maximum_add_fusion
  439.0 23.5 %conditional.10 = (bf16[2,1024,767]{1,2,0:T(8,128)(2,1)}, f32[768,3072]{1,0:T(8,128)}, f32[3072,768]{1,0:T(8,128)}, f32[]{:T(128)}, f32[]{:T(128)}, /*index=5*/b...) conditional(s32[]{:T(128)} %convert_element_type.231, (bf16[2,1024,767]{1,0,2:T(2,128)(2,1)}, ...), branch_computations={%region_45.55_spmd, %region_55.56_spmd} | conditional | flops 29146730496 | bytes 256399584 | solution.py:306
  454.4 6.8 copy.90
  463.8 37.0 %collective-permute-done.3 = bf16[1024,767]{0,1:T(8,128)(2,1)S(1)} collective-permute-done((bf16[1024,767]{0,1:T(8,128)(2,1)}, bf16[1024,767]{0,1:T(8,128)(2,1)S(1)}, u32[]{:S(2)}, u32[]{:S(2)}) %collective-permute-start.3) | collective-permute-done | bytes 1570848 | tf_op jit(solution)/shard_map/ppermute | solution.py:19
  500.8 168.5 %conditional.11 = (f32[768,3072]{1,0:T(8,128)}, bf16[1,2,1024,767]{2,1,3,0:T(2,128)(2,1)}) conditional(s32[]{:T(128)} %convert_element_type.231, (bf16[2,1024,767]{1,2,0:T(8,128)(2,1)}, f32[768,3072]{1,0:T(8,128)}) %tuple.169, (bf16[2,1024,767]{1,0,2:T(2,128)(2,1)S(1)}, s32[2,1024]{1,0:T(2,128)S(1)}, bf16[2,1024,2304]{2,1,0:T(8,128)(2,1)}, ...), branch_computations={%region_56.57_spmd, %region_57.64_spmd} | conditional | flops 15912253440 | bytes 623071744 | solution.py:306
  508.3 4.8 copy.76
  513.2 5.2 convolution_bitcast_fusion.1
  518.4 12.7 %copy.75 = bf16[2,1024,2304]{1,2,0:T(8,128)(2,1)} copy(bf16[2,1024,2304]{2,1,0:T(8,128)(2,1)} %get-tuple-element.688) | data formatting | bytes 18874368 | tf_op jit(solution)/shard_map
  538.2 4.0 fusion.94
  542.3 6.8 multiply_reduce_fusion.7
  549.1 7.0 multiply_convert_fusion.11
  561.3 10.3 fusion.177
  571.6 12.8 %fusion.84 = bf16[1024,12,64]{0,2,1:T(8,128)(2,1)} fusion(f32[512,12,64]{0,2,1:T(8,128)S(1)} %copy-done.71, bf16[512,12,64]{0,2,1:T(8,128)(2,1)S(1)} %bitcast.302, f32[12,512,1024]{2,1,0:T(8,128)} %fusion.177, f32[12,512]{1,0:T(8,128)S(1)} %get-tuple-element.757, pred[512,1024]{1,0:T(8,128)(4,1)S(1)} %copy-done.41), kind=kOutput, calls=%fused_computation.182 | convolution fusion | flops 832045056 | bytes 29646848 | tf_op jit(solution)/shard_map/cond/branch_1_fun/hqk,qhd->khd/dot_general | solution.py:140
  584.4 18.2 %multiply_reduce_fusion.6 = (f32[12,512]{1,0:T(8,128)S(1)}, f32[12,512,1024]{2,1,0:T(8,128)}) fusion(f32[12,512,1024]{2,1,0:T(8,128)} %fusion.177, f32[12,512]{1,0:T(8,128)S(1)} %get-tuple-element.757, pred[512,1024]{1,0:T(8,128)(4,1)} %fusion.86, bf16[512,12,64]{0,2,1:T(8,128)(2,1)} %bitcast.301, bf16[1024,12,64]{0,2,1:T(8,128)(2,1)} %bitcast.280), kind=kOutput, calls=%fused_computation.161 | convolution fusion | flops 836757504 | bytes 53264384 | tf_op jit(solution)/shard_map/cond/branch_1_fun/qhd,khd->hqk/dot_general | solution.py:142
  602.6 18.3 %multiply_convert_fusion.10 = bf16[12,512,1024]{2,1,0:T(8,128)(2,1)S(1)} fusion(f32[12,512,1024]{2,1,0:T(8,128)} %get-tuple-element.764, f32[12,512,1024]{2,1,0:T(8,128)} %fusion.177, f32[12,512]{1,0:T(8,128)S(1)} %get-tuple-element.763, f32[12,512]{1,0:T(8,128)S(1)} %get-tuple-element.757, pred[512,1024]{1,0:T(8,128)(4,1)} %fusion.86), kind=kLoop, calls=%fused_computation.160 | loop fusion | flops 37748736 | bytes 63488000 | tf_op jit(solution)/shard_map/cond/branch_1_fun/convert_element_type | solution.py:148
  620.9 4.6 copy-done.4
  625.5 3.5 fusion.85
  629.0 9.8 fusion.97
  641.1 5.8 multiply_reduce_fusion.8
  647.8 3.9 fusion.88
  651.6 8.9 maximum_add_fusion.1
  662.3 6.8 copy.92
  669.3 330.6 %all-reduce.17.cloned.1.call-done = (f32[1,768,3072]{2,1,0:T(8,128)}, f32[3072,768]{1,0:T(8,128)}) async-done(((f32[1,768,3072]{2,1,0:T(8,128)}, f32[3072,768]{1,0:T(8,128)}), (f32[1,768,3072]{2,1,0:T(8,128)}, f32[3072,768]{1,0:T(8,128)})) %all-reduce.17.cloned.1.call-update) | async-done | bytes 18874384 | tf_op jit(solution)/shard_map/psum | solution.py:331
  1003.8 34.1 %all-reduce.13 = (f32[]{:T(128)}, f32[]{:T(128)}) all-reduce(f32[]{:T(128)} %get-tuple-element.582, f32[]{:T(128)} %get-tuple-element.583), channel_id=1, replica_groups=mesh['section'=2,'dp'=16] {'dp'}, use_global_device_ids=true, to_apply=%region_66.67 | all-reduce | flops 2 | bytes 16 | tf_op jit(solution)/shard_map/psum | solution.py:331
  1040.5 16.8 %collective-permute-done.4 = bf16[1536,768]{1,0:T(8,128)(2,1)} collective-permute-done((bf16[1536,768]{1,0:T(8,128)(2,1)S(1)}, bf16[1536,768]{1,0:T(8,128)(2,1)}, u32[]{:S(2)}, u32[]{:S(2)}) %collective-permute-start.4) | collective-permute-done | bytes 2359328 | tf_op jit(solution)/shard_map/ppermute | solution.py:19
  1057.4 5.7 slice_select_fusion
  1063.1 3.7 copy.170
  (262 shorter events, 157.9 us)
Async XLA Ops:
  7.2 992.7 %all-reduce.17.cloned.1.call-start = ((), (), s32[]{:S(2)}) async-start(), calls=%async_computation | async-start | bytes 37748736 | tf_op jit(solution)/shard_map/psum | solution.py:331
  9.6 4.2 copy-start.67
  18.5 2.0 copy-start.46
  25.0 3.1 copy-start.11
  59.0 5.6 copy-start.37
  59.0 5.6 copy-start.44
  59.0 5.6 copy-start.47
  64.6 10.8 %copy-start.45 = (pred[512,1024]{1,0:T(8,128)(4,1)S(1)}, pred[512,1024]{1,0:T(8,128)(4,1)}, u32[]{:S(2)}) copy-start(pred[512,1024]{1,0:T(8,128)(4,1)} %fusion.9) | copy-start | bytes 1572868 | tf_op jit(solution)/shard_map/cond
  75.4 15.4 %copy-start.1 = (f32[12,512,1024]{2,1,0:T(8,128)S(1)}, f32[12,512,1024]{2,1,0:T(8,128)}, u32[]{:S(2)}) copy-start(f32[12,512,1024]{2,1,0:T(8,128)} %get-tuple-element.776) | copy-start | bytes 75497472 | tf_op jit(solution)/shard_map/cond
  100.4 1.7 copy-start.57
  102.2 8.0 slice-start
  102.2 8.0 slice-start.1
  106.3 3.9 slice-start.2
  111.7 36.2 %copy-start = (bf16[2,1024,2304]{2,1,0:T(8,128)(2,1)}, bf16[2,1024,2304]{2,1,0:T(8,128)(2,1)S(1)}, u32[]{:S(2)}) copy-start(bf16[2,1024,2304]{2,1,0:T(8,128)(2,1)S(1)} %get-tuple-element.557) | copy-start | bytes 28311556
  111.7 36.1 %collective-permute-start = (bf16[1024,767]{0,1:T(8,128)(2,1)}, bf16[1024,767]{0,1:T(8,128)(2,1)S(1)}, u32[]{:S(2)}, u32[]{:S(2)}) collective-permute-start(bf16[1024,767]{0,1:T(8,128)(2,1)} %get-tuple-element.552), channel_id=1, source_target_pairs={{0,16},{1,17},{2,18},{3,19},{4,20},{5,21},{6,22},{7,23},{8,24},{9,... | collective-permute-start | bytes 4712456 | tf_op jit(solution)/shard_map/ppermute | solution.py:19
  164.4 3.6 copy-start.31
  164.4 111.8 %collective-permute-start.2 = (bf16[1024,767]{0,1:T(8,128)(2,1)}, bf16[1024,767]{0,1:T(8,128)(2,1)}, u32[]{:S(2)}, u32[]{:S(2)}) collective-permute-start(bf16[1024,767]{0,1:T(8,128)(2,1)} %get-tuple-element.565), channel_id=1, source_target_pairs={{16,0},{17,1},{18,2},{19,3},{20,4},{21,5},{22,6},{23,7},{24,8},{25... | collective-permute-start | bytes 4712456 | tf_op jit(solution)/shard_map/ppermute | solution.py:19
  173.0 1.8 copy-start.12
  219.9 5.7 copy-start.36
  219.9 5.7 copy-start.42
  219.9 5.7 copy-start.48
  225.6 10.6 copy-start.43
  236.2 15.4 %copy-start.2 = (f32[12,512,1024]{2,1,0:T(8,128)S(1)}, f32[12,512,1024]{2,1,0:T(8,128)}, u32[]{:S(2)}) copy-start(f32[12,512,1024]{2,1,0:T(8,128)} %get-tuple-element.792) | copy-start | bytes 75497472 | tf_op jit(solution)/shard_map/cond
  251.6 9.9 copy-start.61
  261.4 2.1 copy-start.22
  261.4 2.2 copy-start.62
  261.5 2.5 copy-start.58
  263.9 2.8 copy-start.13
  268.6 4.6 copy-start.64
  273.7 2.5 copy-start.65
  273.7 165.3 %collective-permute-start.1 = (bf16[1024,767]{0,1:T(8,128)(2,1)}, bf16[1024,767]{0,1:T(8,128)(2,1)}, u32[]{:S(2)}, u32[]{:S(2)}) collective-permute-start(bf16[1024,767]{0,1:T(8,128)(2,1)} %get-tuple-element.562), channel_id=1, source_target_pairs={{0,16},{1,17},{2,18},{3,19},{4,20},{5,21},{6,22},{7,23},{8,24},{9,... | collective-permute-start | bytes 4712456 | tf_op jit(solution)/shard_map/ppermute | solution.py:19
  277.9 2.1 copy-start.59
  281.4 2.5 copy-start.8
  313.1 1.8 copy-start.49
  337.1 10.3 copy-start.40
  337.1 10.3 copy-start.51
  337.1 10.3 copy-start.70
  378.4 22.3 %copy-start.38 = (f32[512,12,64]{0,2,1:T(8,128)S(1)}, f32[512,12,64]{0,2,1:T(8,128)}, u32[]{:S(2)}) copy-start(f32[512,12,64]{0,2,1:T(8,128)} %multiply_bitcast_fusion) | copy-start | bytes 4718596 | tf_op jit(solution)/shard_map/cond
  396.1 4.6 copy-start.3
  412.7 1.9 copy-start.10
  421.2 1.9 copy-start.68
  423.1 3.9 copy-start.55
  439.0 61.8 %copy-start.7 = (bf16[2,1024,767]{1,0,2:T(2,128)(2,1)S(1)}, bf16[2,1024,767]{1,0,2:T(2,128)(2,1)}, u32[]{:S(2)}) copy-start(bf16[2,1024,767]{1,0,2:T(2,128)(2,1)} %param.69) | copy-start | bytes 9424900
  439.0 61.8 %copy-start.66 = (f32[2,12,1024]{2,1,0:T(8,128)S(1)}, f32[2,12,1024]{2,1,0:T(8,128)}, u32[]{:S(2)}) copy-start(f32[2,12,1024]{2,1,0:T(8,128)} %copy-done.65) | copy-start | bytes 294916
  462.6 38.3 %collective-permute-start.3 = (bf16[1024,767]{0,1:T(8,128)(2,1)}, bf16[1024,767]{0,1:T(8,128)(2,1)S(1)}, u32[]{:S(2)}, u32[]{:S(2)}) collective-permute-start(bf16[1024,767]{0,1:T(8,128)(2,1)} %get-tuple-element.577), channel_id=1, source_target_pairs={{16,0},{17,1},{18,2},{19,3},{20,4},{21,5},{22,6},{23,7},{24,8},{25... | collective-permute-start | bytes 4712456 | tf_op jit(solution)/shard_map/ppermute | solution.py:19
  500.8 2.3 copy-start.34
  502.9 2.3 copy-start.20
  534.2 2.2 copy-start.32
  534.2 27.0 %copy-start.14 = (bf16[512,768]{0,1:T(8,128)(2,1)}, bf16[512,768]{0,1:T(8,128)(2,1)S(1)}, u32[]{:S(2)}) copy-start(bf16[512,768]{0,1:T(8,128)(2,1)S(1)} %get-tuple-element.752) | copy-start | bytes 2359300 | tf_op jit(solution)/shard_map/cond
  536.4 1.8 copy-start.50
  556.1 2.0 copy-start.33
  558.1 3.1 copy-start.16
  561.3 10.3 copy-start.41
  561.3 10.3 copy-start.52
  561.3 10.3 copy-start.71
  602.6 22.9 %copy-start.15 = (bf16[512,768]{0,1:T(8,128)(2,1)S(1)}, bf16[512,768]{0,1:T(8,128)(2,1)}, u32[]{:S(2)}) copy-start(bf16[512,768]{0,1:T(8,128)(2,1)} %copy-done.14) | copy-start | bytes 2359300 | tf_op jit(solution)/shard_map/cond
  602.6 22.9 %copy-start.39 = (f32[512,12,64]{0,2,1:T(8,128)S(1)}, f32[512,12,64]{0,2,1:T(8,128)}, u32[]{:S(2)}) copy-start(f32[512,12,64]{0,2,1:T(8,128)} %multiply_bitcast_fusion.1) | copy-start | bytes 4718596 | tf_op jit(solution)/shard_map/cond
  620.9 4.6 copy-start.4
  638.8 1.9 copy-start.54
  638.8 2.4 copy-start.69
  647.7 3.9 copy-start.56
  651.6 9.0 copy-start.35
  1002.5 54.9 %collective-permute-start.4 = (bf16[1536,768]{1,0:T(8,128)(2,1)S(1)}, bf16[1536,768]{1,0:T(8,128)(2,1)}, u32[]{:S(2)}, u32[]{:S(2)}) collective-permute-start(bf16[1536,768]{1,0:T(8,128)(2,1)S(1)} %slice.908), channel_id=1, source_target_pairs={{16,0},{17,1},{18,2},{19,3},{20,4},{21,5},{22,6},{23,7},{24,8},{25... | collective-permute-start | bytes 7077896 | tf_op jit(solution)/shard_map/ppermute | solution.py:19
  1040.5 22.6 %copy-start.30 = (f32[1,768,3072]{2,1,0:T(8,128)S(1)}, f32[1,768,3072]{2,1,0:T(8,128)}, u32[]{:S(2)}) copy-start(f32[1,768,3072]{2,1,0:T(8,128)} %get-tuple-element.875) | copy-start | bytes 28311556
  (7 other events, 10.9 us)
Sparse Core Ops, SparseCore 0:
  669.5 330.3 all-reduce.16
where the time goes:
time: 1080 us
  waiting for transfers between devices  419 us (39%)
  matrix products  251 us (23%)
  local copies, waits for them, and re-layouts  184 us (17%)
  other arithmetic  133 us (12%)
  blocking collectives  34.1 us (3%)
  loops' own time  27.5 us (3%)
  between operations  19.3 us (2%)
    psum x1, waiting for transfers between devices, on_device(): lax.psum((first_sum, down_sum, carried[7], carried[8]), 'dp')  331 us
    ppermute x5, waiting for transfers between devices, shifted(): return lax.ppermute(block, axis, route)  88.6 us
    cond x121, local copies, waits for them, and re-layouts  53.4 us
    dot_general x4, matrix products, attend_back(): jnp.einsum('qhd,khd->hqk', grad_block, values[:reach], preferred_element_...  50 us
    convert_element_type x4, other arithmetic, attend_back(): grad_low = grad_scores.astype(jnp.bfloat16)  50 us
    another operation x9, local copies, waits for them, and re-layouts  42.9 us
    psum x1, blocking collectives, on_device(): lax.psum((first_sum, down_sum, carried[7], carried[8]), 'dp')  34.1 us
    dot_general x4, matrix products, attend_back(): jnp.einsum('hqk,qhd->khd', probs_low, grad_block, preferred_element_type=...  33.7 us
  transfers between devices with their start and end apart: 6, of which 4 were waited for; matrix products, arithmetic and copies ran while one was open for 23% of the time, Pallas kernels for 0%

commit v1 on v0

v1 whole, which is shorter than its diff:
```python
import functools

import jax
import jax.numpy as jnp
from jax import lax
from jax.experimental import pallas as pl
from jax.experimental.pallas import tpu as pltpu
from jax.sharding import PartitionSpec as P

HEADS = 12
HEAD_DIM = 64
GROUPS = 3
EPSILON = 1e-06
MASKED = -1e30
SCALE = HEAD_DIM ** (-0.5)
LOG2E = 1.4426950408889634
LOW = jnp.bfloat16
FULL = jnp.float32
VMEM = 58 * 2**20


def dot(left, right, left_dim=1, right_dim=0):
    return lax.dot_general(
        left, right, (((left_dim,), (right_dim,)), ((), ())), preferred_element_type=FULL
    )


def kernel_call(body, name, grid_spec, out_shape, flops, moved, exps=0, aliases=None):
    return pl.pallas_call(
        body,
        grid_spec=grid_spec,
        out_shape=out_shape,
        input_output_aliases=aliases or {},
        compiler_params=pltpu.CompilerParams(vmem_limit_bytes=VMEM),
        cost_estimate=pl.CostEstimate(flops=int(flops), bytes_accessed=int(moved), transcendentals=int(exps)),
        name=name,
    )


def widened(block):
    lane = lax.broadcasted_iota(jnp.int32, block.shape, 1)
    last = block.shape[1] - 1
    values = jnp.where(lane == last, 0.0, block.astype(FULL))
    return jnp.where(lane == last, -jnp.sum(values, axis=1, keepdims=True), values)


def crms(values):
    inverse = lax.rsqrt(jnp.mean(values * values, axis=1, keepdims=True) + EPSILON)
    return values * inverse, inverse


def crms_back(normed, inverse, grad):
    return inverse * (grad - normed * jnp.mean(grad * normed, axis=1, keepdims=True))


def compressed(branch):
    return branch - jnp.mean(branch, axis=1, keepdims=True)


def widened_back(grad):
    last = grad.shape[1] - 1
    return grad - grad[:, last:]


def compressed_back(block):
    lane = lax.broadcasted_iota(jnp.int32, block.shape, 1)
    values = jnp.where(lane == block.shape[1] - 1, 0.0, block.astype(FULL))
    return values - jnp.mean(values, axis=1, keepdims=True)


def square_sum(rounded, valid_row):
    wide = widened(rounded)
    per_token = jnp.sum(wide * wide, axis=1, keepdims=True)
    tokens = valid_row.shape[1]
    valid = jnp.transpose(jnp.broadcast_to(valid_row, (128, tokens)))[:, :1]
    return jnp.sum(jnp.where(valid > 0.5, per_token, 0.0), axis=0, keepdims=True)


def prep_kernel(where_ref, x_ref, cot_ref, nt_ref, g_ref):
    normed, _ = crms(widened(x_ref[0]))
    nt_ref[...] = jnp.transpose(normed.astype(LOW))
    g_ref[...] = compressed_back(cot_ref[0]).astype(LOW)


def prep(where, stream_in, cotangent):
    length, width = stream_in.shape[1], stream_in.shape[2] + 1
    block = length // 4
    return kernel_call(
        prep_kernel,
        "prep",
        pltpu.PrefetchScalarGridSpec(
            num_scalar_prefetch=1,
            grid=(4,),
            in_specs=[
                pl.BlockSpec((1, block, width), lambda t, w: (w[0], t, 0)),
                pl.BlockSpec((1, block, width), lambda t, w: (w[0], t, 0)),
            ],
            out_specs=[
                pl.BlockSpec((width, block), lambda t, w: (0, t)),
                pl.BlockSpec((block, width), lambda t, w: (t, 0)),
            ],
        ),
        [jax.ShapeDtypeStruct((width, length), LOW), jax.ShapeDtypeStruct((length, width), LOW)],
        0,
        8 * length * width,
    )(where, stream_in, cotangent)


def branch_grad_kernel(g_ref, w_ref, out_ref):
    out_ref[0] = dot(g_ref[...], w_ref[...], 1, 1).astype(LOW)


def branch_grad(g, down_weight):
    length, width = g.shape
    blocks = down_weight.shape[0] // width
    return kernel_call(
        branch_grad_kernel,
        "branch_grad",
        pltpu.PrefetchScalarGridSpec(
            num_scalar_prefetch=0,
            grid=(blocks,),
            in_specs=[
                pl.BlockSpec((length, width), lambda b: (0, 0)),
                pl.BlockSpec((width, width), lambda b: (b, 0)),
            ],
            out_specs=pl.BlockSpec((1, length, width), lambda b: (b, 0, 0)),
        ),
        jax.ShapeDtypeStruct((blocks, length, width), LOW),
        2 * length * width * width * blocks,
        2 * length * width * (blocks + 1),
    )(g, down_weight)


def own_column(group, piece, section):
    attention = jnp.where(group < GROUPS, group + GROUPS * piece, 3 * GROUPS + piece)
    return jnp.where(section == 0, attention, 3 * group + piece)


def own_column_static(group, piece, section):
    if section == 1 or group == GROUPS:
        return 3 * group + piece
    return group + GROUPS * piece


def piece_kernel(where_ref, w_ref, out_ref):
    out_ref[0] = w_ref[0]


def weight_piece(where, weights):
    rows, columns = weights.shape[1:]
    part = columns // 12
    return kernel_call(
        piece_kernel,
        "weight_piece",
        pltpu.PrefetchScalarGridSpec(
            num_scalar_prefetch=1,
            grid=(4, 3),
            in_specs=[pl.BlockSpec((1, rows // 4, part), lambda g, j, w: (0, w[1], own_column(g, j, w[0])))],
            out_specs=pl.BlockSpec((1, rows // 4, part), lambda g, j, w: (g, 0, j)),
        ),
        jax.ShapeDtypeStruct((4, rows // 4, 3 * part), LOW),
        0,
        rows * columns,
    )(where, weights)


def weight_copies(group, wanted, where_ref, own_ref, near_ref, beside_ref, core_ref, target, sem, act):
    quarter = target.shape[0] // 4
    part = target.shape[1] // 3

    @pl.when(where_ref[0] == wanted)
    def _():
        for piece in range(3):
            column = own_column_static(group, piece, wanted) * part
            act(pltpu.make_async_copy(own_ref.at[0, :, pl.ds(column, part)], target.at[:, pl.ds(piece * part, part)], sem.at[piece]))

    @pl.when(where_ref[0] != wanted)
    def _():
        sources = (near_ref, beside_ref, core_ref.at[0], core_ref.at[1])
        for place, source in enumerate(sources):
            index = where_ref[1] ^ (0, 2, 1, 3)[place]
            act(pltpu.make_async_copy(source, target.at[pl.ds(index * quarter, quarter), :], sem.at[place]))


def segment_rows(segment):
    tokens = segment.shape[1]
    ids = lax.broadcasted_iota(jnp.int32, (16, tokens), 0)
    same = segment == ids
    real = ids < 5
    queries = jnp.where(real & jnp.logical_not(same), MASKED, 0.0).astype(LOW)
    keys = jnp.where(real & same, 1.0, 0.0).astype(LOW)
    return queries, keys


def two_parts(values):
    high = values.astype(LOW)
    return high, (values - high.astype(FULL)).astype(LOW)


def minus_rows(values):
    high = values.astype(LOW)
    rest = values - high.astype(FULL)
    middle = rest.astype(LOW)
    low = rest - middle.astype(FULL)
    row = lax.broadcasted_iota(jnp.int32, (16, values.shape[1]), 0)
    parts = jnp.where(
        row == 0, high.astype(FULL), jnp.where(row == 1, middle.astype(FULL), jnp.where(row == 2, low, 0.0))
    )
    return (-parts).astype(LOW)


def three_ones(tokens):
    return jnp.where(lax.broadcasted_iota(jnp.int32, (16, tokens), 0) < 3, 1.0, 0.0).astype(LOW)


def head_tasks(heads, blocks, block):
    return [
        (head, slice(i * block, (i + 1) * block), slice(0, (i + 1) * block), i * block)
        for head in range(heads)
        for i in range(blocks)
    ]


def in_stages(tasks, stages):
    for step in range(len(tasks) + len(stages) - 1):
        for late, stage in enumerate(stages):
            if 0 <= step - late < len(tasks):
                stage(tasks[step - late])


def attend_kernel(group, where_ref, own_ref, near_ref, beside_ref, core_ref, nt_ref, seg_ref, qkv_ref, mixed_ref, total_ref, w_ref, sem):
    copies = functools.partial(
        weight_copies, group, 0, where_ref, own_ref, near_ref, beside_ref, core_ref, w_ref, sem
    )
    copies(lambda c: c.start())
    copies(lambda c: c.wait())
    length = nt_ref.shape[1]
    width = qkv_ref.shape[0] // 3
    heads, blocks = width // HEAD_DIM, 4
    block = length // blocks
    for part in range(3):
        qkv_ref[part * width : (part + 1) * width, :] = dot(
            w_ref[:, part * width : (part + 1) * width], nt_ref[...], 0, 0
        ).astype(LOW)
    seg_queries, seg_keys = segment_rows(seg_ref[0])
    causal = lax.broadcasted_iota(jnp.int32, (block, block), 0) <= lax.broadcasted_iota(jnp.int32, (block, block), 1)
    ones = three_ones(length)
    scored, weighed = {}, {}

    def score(task):
        head, queries, keys, _ = task
        high, low = two_parts(qkv_ref[head * HEAD_DIM : (head + 1) * HEAD_DIM, queries].astype(FULL) * (SCALE * LOG2E))
        key_rows = qkv_ref[width + head * HEAD_DIM : width + (head + 1) * HEAD_DIM, keys]
        scored[task] = dot(
            jnp.concatenate([key_rows, key_rows, seg_keys[:, keys]], axis=0),
            jnp.concatenate([high, low, seg_queries[:, queries]], axis=0),
            0,
            0,
        )

    def weigh(task):
        before = task[3]
        scores = scored.pop(task)
        last = jnp.where(causal, scores[before:], MASKED)
        highest = jnp.max(last, axis=0, keepdims=True)
        if before:
            highest = jnp.maximum(highest, jnp.max(scores[:before], axis=0, keepdims=True))
        exponents = jnp.exp2(last - highest).astype(LOW)
        if before:
            exponents = jnp.concatenate([jnp.exp2(scores[:before] - highest).astype(LOW), exponents], axis=0)
        weighed[task] = (exponents, highest)

    def mix(task):
        head, queries, keys, _ = task
        exponents, highest = weighed.pop(task)
        values = qkv_ref[2 * width + head * HEAD_DIM : 2 * width + (head + 1) * HEAD_DIM, keys]
        mixed = dot(jnp.concatenate([values, ones[:, keys]], axis=0), exponents)
        total = mixed[HEAD_DIM : HEAD_DIM + 1]
        mixed_ref[head * HEAD_DIM : (head + 1) * HEAD_DIM, queries] = (mixed[:HEAD_DIM] / total).astype(LOW)
        total_ref[head : head + 1, queries] = highest + jnp.log2(total)

    in_stages(head_tasks(heads, blocks, block), (score, weigh, mix))


def attend(group, where, own, received, nt, segments):
    width, length = nt.shape
    part = width // GROUPS
    anywhere = pl.BlockSpec(memory_space=pl.ANY)
    return kernel_call(
        functools.partial(attend_kernel, group),
        "attend",
        pltpu.PrefetchScalarGridSpec(
            num_scalar_prefetch=1,
            grid=(1,),
            in_specs=[anywhere] * 4
            + [
                pl.BlockSpec((width, length), lambda i, w: (0, 0)),
                pl.BlockSpec((1, 1, length), lambda i, w: (w[0], 0, 0)),
            ],
            out_specs=[
                pl.BlockSpec((3 * part, length), lambda i, w: (0, 0)),
                pl.BlockSpec((part, length), lambda i, w: (0, 0)),
                pl.BlockSpec((part // HEAD_DIM, length), lambda i, w: (0, 0)),
                pl.BlockSpec((width, 3 * part), lambda i, w: (0, 0)),
            ],
            scratch_shapes=[pltpu.SemaphoreType.DMA((4,))],
        ),
        [
            jax.ShapeDtypeStruct((3 * part, length), LOW),
            jax.ShapeDtypeStruct((part, length), LOW),
            jax.ShapeDtypeStruct((part // HEAD_DIM, length), FULL),
            jax.ShapeDtypeStruct((width, 3 * part), LOW),
        ],
        4.5e9,
        8 * width * length,
    )(where, own, *received, nt, segments)


def attend_back_kernel(qkv_ref, gm_ref, total_ref, delta_ref, seg_ref, w_ref, nt_ref, *rest):
    before_refs, (gw_ref, gn_ref, acc) = rest[:-3], rest[-3:]
    length = nt_ref.shape[1]
    width = gm_ref.shape[0]
    heads, blocks = width // HEAD_DIM, 4
    block = length // blocks
    seg_queries, seg_keys = segment_rows(seg_ref[0])
    ones = three_ones(length)
    causal = lax.broadcasted_iota(jnp.int32, (block, block), 1) <= lax.broadcasted_iota(jnp.int32, (block, block), 0)
    acc[...] = jnp.zeros_like(acc)
    scored, weighed = {}, {}

    def rows(part, head):
        return slice(part * width + head * HEAD_DIM, part * width + (head + 1) * HEAD_DIM)

    def score(task):
        head, queries, keys, _ = task
        high, low = two_parts(qkv_ref[rows(0, head), queries].astype(FULL) * (SCALE * LOG2E))
        key_rows = qkv_ref[rows(1, head), keys]
        scores = dot(
            jnp.concatenate([high, low, seg_queries[:, queries], minus_rows(total_ref[head : head + 1, queries])], axis=0),
            jnp.concatenate([key_rows, key_rows, seg_keys[:, keys], ones[:, keys]], axis=0),
            0,
            0,
        )
        grads = dot(
            jnp.concatenate([gm_ref[rows(0, head), queries], minus_rows(delta_ref[head : head + 1, queries])], axis=0),
            jnp.concatenate([qkv_ref[rows(2, head), keys], ones[:, keys]], axis=0),
            0,
            0,
        )
        scored[task] = (scores, grads)

    def weigh(task):
        before = task[3]
        scores, grads = scored.pop(task)
        last = jnp.where(causal, scores[:, before:], MASKED)
        if before:
            last = jnp.concatenate([scores[:, :before], last], axis=1)
        probs = jnp.exp2(last)
        weighed[task] = (probs.astype(LOW), (probs * grads).astype(LOW))

    def collect(task):
        head, queries, keys, _ = task
        probs, grads = weighed.pop(task)
        acc[rows(2, head), keys] += dot(gm_ref[rows(0, head), queries], probs)
        acc[rows(1, head), keys] += dot(qkv_ref[rows(0, head), queries] * LOW(SCALE), grads)
        acc[rows(0, head), queries] = dot(qkv_ref[rows(1, head), keys], grads, 1, 1) * SCALE

    in_stages(head_tasks(heads, blocks, block), (score, weigh, collect))
    grads = acc[...].astype(LOW)
    gw_ref[...] = dot(nt_ref[...], grads, 1, 1).astype(LOW)
    grad_normed = dot(w_ref[...], grads)
    if before_refs:
        grad_normed = grad_normed + before_refs[0][...]
    gn_ref[...] = grad_normed


def attend_back(where, qkv, gm, total, delta, segments, w, nt, before=None):
    width, length = nt.shape
    part = gm.shape[0]
    whole = lambda a: pl.BlockSpec(a.shape, lambda i, w: (0,) * a.ndim)
    arrays = [qkv, gm, total, delta]
    extra = [] if before is None else [before]

    def body(where_ref, *refs):
        attend_back_kernel(*refs)

    return kernel_call(
        body,
        "attend_back",
        pltpu.PrefetchScalarGridSpec(
            num_scalar_prefetch=1,
            grid=(1,),
            in_specs=[whole(a) for a in arrays]
            + [pl.BlockSpec((1, 1, length), lambda i, w: (w[0], 0, 0)), whole(w), whole(nt)]
            + [whole(a) for a in extra],
            out_specs=[
                pl.BlockSpec((width, 3 * part), lambda i, w: (0, 0)),
                pl.BlockSpec((width, length), lambda i, w: (0, 0)),
            ],
            scratch_shapes=[pltpu.VMEM((3 * part, length), FULL)],
        ),
        [jax.ShapeDtypeStruct((width, 3 * part), LOW), jax.ShapeDtypeStruct((width, length), FULL)],
        9e9,
        8 * width * length,
    )(where, *arrays, segments, w, nt, *extra)


def middle_kernel(where_ref, own_ref, near_ref, beside_ref, core_ref, *refs):
    mixed_refs, (x_ref, seg_ref, mid_ref, nm_ref, nmt_ref, sums_ref, w_ref, sem) = refs[:GROUPS], refs[GROUPS:]
    step = pl.program_id(0)

    @pl.when(step == 0)
    def _():
        copies = functools.partial(
            weight_copies, GROUPS, 0, where_ref, own_ref, near_ref, beside_ref, core_ref, w_ref, sem
        )
        copies(lambda c: c.start())
        copies(lambda c: c.wait())
        sums_ref[...] = jnp.zeros_like(sums_ref)

    mixed = jnp.concatenate([ref[...] for ref in mixed_refs], axis=0)
    branch = dot(mixed, w_ref[...], 0, 0)
    middle = (x_ref[0].astype(FULL) + compressed(branch)).astype(LOW)
    mid_ref[...] = middle
    normed, _ = crms(widened(middle))
    low = normed.astype(LOW)
    nm_ref[...] = low
    nmt_ref[...] = jnp.transpose(low)
    valid = (seg_ref[0] > 0).astype(FULL)
    lane = lax.broadcasted_iota(jnp.int32, sums_ref.shape, 1)
    count = jnp.sum(valid, axis=1, keepdims=True)
    sums_ref[...] += jnp.where(lane == 0, square_sum(middle, valid), 0.0) + jnp.where(lane == 2, count, 0.0)


def middle_of(where, own, received, mixed, stream_in, segments):
    length, width = stream_in.shape[1], stream_in.shape[2] + 1
    block = length // 4
    anywhere = pl.BlockSpec(memory_space=pl.ANY)
    return kernel_call(
        middle_kernel,
        "middle",
        pltpu.PrefetchScalarGridSpec(
            num_scalar_prefetch=1,
            grid=(4,),
            in_specs=[anywhere] * 4
            + [pl.BlockSpec((width // GROUPS, block), lambda t, w: (0, t))] * GROUPS
            + [
                pl.BlockSpec((1, block, width), lambda t, w: (w[0], t, 0)),
                pl.BlockSpec((1, 1, block), lambda t, w: (w[0], 0, t)),
            ],
            out_specs=[
                pl.BlockSpec((block, width), lambda t, w: (t, 0)),
                pl.BlockSpec((block, width), lambda t, w: (t, 0)),
                pl.BlockSpec((width, block), lambda t, w: (0, t)),
                pl.BlockSpec((8, 128), lambda t, w: (0, 0)),
                pl.BlockSpec((width, width), lambda t, w: (0, 0)),
            ],
            scratch_shapes=[pltpu.SemaphoreType.DMA((4,))],
        ),
        [
            jax.ShapeDtypeStruct((length, width - 1), LOW),
            jax.ShapeDtypeStruct((length, width), LOW),
            jax.ShapeDtypeStruct((width, length), LOW),
            jax.ShapeDtypeStruct((8, 128), FULL),
            jax.ShapeDtypeStruct((width, width), LOW),
        ],
        2 * length * width * width,
        12 * length * width,
    )(where, own, *received, *mixed, stream_in, segments)


def gelu_both(hidden):
    rate = 0.7978845608028654
    square = hidden * hidden
    tanh = jnp.tanh(rate * hidden * (1.0 + 0.044715 * square))
    half = 0.5 + 0.5 * tanh
    slope = half + (0.5 * rate) * hidden * (1.0 - tanh * tanh) * (1.0 + (3 * 0.044715) * square)
    return hidden * half, slope


def feed_kernel(where_ref, own_ref, *refs):
    received, refs = refs[:12], refs[12:]
    (nm_ref, nmt_ref, g_ref, ga_ref, down_ref, mid_ref, cot_ref, seg_ref) = refs[:8]
    (keep_dn, send_dn, keep_up, send_up, keep_out, send_out, gmid_ref, gab_ref, sums_ref) = refs[8:17]
    (weights, act, slope_grad, out_acc, gn_acc, sem) = refs[17:]
    step, steps = pl.program_id(0), pl.num_programs(0)
    length, width = nm_ref.shape
    blocks = 4
    block = length // blocks

    def copies(group, do):
        weight_copies(
            group, 1, where_ref, own_ref, *received[3 * group : 3 * group + 3], weights.at[group], sem.at[group], do
        )

    @pl.when(step == 0)
    def _():
        for group in range(4):
            copies(group, lambda c: c.start())
        out_acc[...] = jnp.zeros_like(out_acc)
        gn_acc[...] = jnp.zeros_like(gn_acc)

    for group in range(4):

        @pl.when(step == group)
        def _(group=group):
            copies(group, lambda c: c.wait())

    up = weights.at[step]
    hidden, waiting = {}, {}

    def enter(rows):
        hidden[rows] = dot(nm_ref[rows, :], up[...])

    def bend(rows):
        value, slope = gelu_both(hidden.pop(rows))
        act[rows, :] = value.astype(LOW)
        slope_grad[rows, :] = (ga_ref[0, rows, :].astype(FULL) * slope).astype(LOW)

    def leave(rows):
        out_acc[rows, :] += dot(act[rows, :], down_ref[...])
        gn_acc[rows, :] += dot(slope_grad[rows, :], up[...], 1, 1)

    in_stages([slice(i * block, (i + 1) * block) for i in range(blocks)], (enter, bend, leave))
    half = width // 2
    mine = pl.multiple_of(where_ref[2] * half, half)
    theirs = pl.multiple_of((1 - where_ref[2]) * half, half)
    keep_dn[0] = dot(act[:, pl.ds(mine, half)], g_ref[...], 0, 0).astype(LOW)
    send_dn[0] = dot(act[:, pl.ds(theirs, half)], g_ref[...], 0, 0).astype(LOW)
    keep_up[0] = dot(nmt_ref[pl.ds(mine, half), :], slope_grad[...]).astype(LOW)
    send_up[0] = dot(nmt_ref[pl.ds(theirs, half), :], slope_grad[...]).astype(LOW)

    @pl.when(step == steps - 1)
    def _():
        on_attention = where_ref[0] == 0
        sums = jnp.zeros((1, 1), FULL)
        for i in range(blocks):
            rows = slice(i * block, (i + 1) * block)
            middle = mid_ref[rows, :]
            wide = widened(middle)
            output = (wide + compressed(out_acc[rows, :])).astype(LOW)
            sums = sums + square_sum(output, (seg_ref[0][:, rows] > 0).astype(FULL))
            keep_out[rows, :] = jnp.where(on_attention, middle, output)
            send_out[rows, :] = jnp.where(on_attention, output, middle)
            normed, inverse = crms(wide)
            grad = (
                cot_ref[0, rows, :].astype(FULL) + widened_back(crms_back(normed, inverse, gn_acc[rows, :]))
            ).astype(LOW)
            gmid_ref[rows, :] = grad
            gab_ref[rows, :] = compressed_back(grad).astype(LOW)
        lane = lax.broadcasted_iota(jnp.int32, sums_ref.shape, 1)
        sums_ref[...] = jnp.where(lane == 1, sums, 0.0)


def feed(where, own, received, nm, nmt, g, ga, down_weight, middle, cotangent, segments):
    length, width = nm.shape
    groups = down_weight.shape[0] // width
    half = width // 2
    anywhere = pl.BlockSpec(memory_space=pl.ANY)
    once = pl.Buffered(1)
    fixed = lambda shape: pl.BlockSpec(shape, lambda b, w: (0,) * len(shape), pipeline_mode=once)
    per_group = lambda *shape: pl.BlockSpec((1, *shape), lambda b, w: (b, 0, 0))
    row = pl.BlockSpec((1, length, width), lambda b, w: (w[0], 0, 0), pipeline_mode=once)
    return kernel_call(
        feed_kernel,
        "feed",
        pltpu.PrefetchScalarGridSpec(
            num_scalar_prefetch=1,
            grid=(groups,),
            in_specs=[anywhere] * 13
            + [
                fixed((length, width)),
                fixed((width, length)),
                fixed((length, width)),
                per_group(length, width),
                pl.BlockSpec((width, width), lambda b, w: (b, 0)),
                fixed((length, width)),
                row,
                pl.BlockSpec((1, 1, length), lambda b, w: (w[0], 0, 0)),
            ],
            out_specs=[per_group(half, width)] * 4
            + [
                fixed((length, width)),
                fixed((length, width)),
                fixed((length, width)),
                fixed((length, width)),
                pl.BlockSpec((8, 128), lambda b, w: (0, 0)),
            ],
            scratch_shapes=[
                pltpu.VMEM((groups, width, width), LOW),
                pltpu.VMEM((length, width), LOW),
                pltpu.VMEM((length, width), LOW),
                pltpu.VMEM((length, width), FULL),
                pltpu.VMEM((length, width), FULL),
                pltpu.SemaphoreType.DMA((groups, 4)),
            ],
        ),
        [jax.ShapeDtypeStruct((groups, half, width), LOW)] * 4
        + [jax.ShapeDtypeStruct((length, width - 1), LOW)] * 3
        + [jax.ShapeDtypeStruct((length, width), LOW), jax.ShapeDtypeStruct((8, 128), FULL)],
        32e9,
        30 * length * width,
    )(where, own, *[a for r in received for a in r], nm, nmt, g, ga, down_weight, middle, cotangent, segments)


def mixed_grad_kernel(gab_ref, w_ref, *refs):
    mixed_refs, (gm_refs, delta_ref, gw_ref) = refs[:GROUPS], (refs[GROUPS : 2 * GROUPS], *refs[2 * GROUPS :])
    gab = gab_ref[...]
    part = gm_refs[0].shape[0]
    heads = part // HEAD_DIM
    for group in range(GROUPS):
        grads = dot(w_ref[group * part : (group + 1) * part, :], gab, 1, 1).astype(LOW)
        gm_refs[group][...] = grads
        mixed = mixed_refs[group][...]
        product = grads.astype(FULL) * mixed.astype(FULL)
        for head in range(heads):
            at = group * heads + head
            delta_ref[at : at + 1, :] = jnp.sum(
                product[head * HEAD_DIM : (head + 1) * HEAD_DIM], axis=0, keepdims=True
            )
        gw_ref[group * part : (group + 1) * part, :] = dot(mixed, gab).astype(LOW)


def mixed_grad(gab, w, mixed):
    length, width = gab.shape
    part = width // GROUPS
    whole = lambda shape: pl.BlockSpec(shape, lambda i: (0,) * len(shape))
    outs = kernel_call(
        mixed_grad_kernel,
        "mixed_grad",
        pltpu.PrefetchScalarGridSpec(
            num_scalar_prefetch=0,
            grid=(1,),
            in_specs=[whole((length, width)), whole((width, width))] + [whole((part, length))] * GROUPS,
            out_specs=[whole((part, length))] * GROUPS + [whole((HEADS, length)), whole((width, width))],
        ),
        [jax.ShapeDtypeStruct((part, length), LOW)] * GROUPS
        + [jax.ShapeDtypeStruct((HEADS, length), FULL), jax.ShapeDtypeStruct((width, width), LOW)],
        4 * length * width * width,
        8 * length * width,
    )(gab, w, *mixed)
    return outs[:GROUPS], outs[GROUPS], outs[GROUPS + 1]


def input_grad_kernel(where_ref, x_ref, gmid_ref, gn_ref, keep_ref, send_ref):
    on_attention = where_ref[0] == 0
    normed, inverse = crms(widened(x_ref[0]))
    middle = gmid_ref[...]
    grad = (
        middle.astype(FULL) + widened_back(crms_back(normed, inverse, jnp.transpose(gn_ref[...])))
    ).astype(LOW)
    keep_ref[...] = jnp.where(on_attention, grad, middle)
    send_ref[...] = jnp.where(on_attention, middle, grad)


def input_grad(where, stream_in, grad_middle, grad_normed):
    length, width = stream_in.shape[1], stream_in.shape[2] + 1
    block = length // 4
    tokens = pl.BlockSpec((block, width), lambda t, w: (t, 0))
    return kernel_call(
        input_grad_kernel,
        "input_grad",
        pltpu.PrefetchScalarGridSpec(
            num_scalar_prefetch=1,
            grid=(4,),
            in_specs=[
                pl.BlockSpec((1, block, width), lambda t, w: (w[0], t, 0)),
                tokens,
                pl.BlockSpec((width, block), lambda t, w: (0, t)),
            ],
            out_specs=[tokens, tokens],
        ),
        [jax.ShapeDtypeStruct((length, width - 1), LOW)] * 2,
        0,
        12 * length * width,
    )(where, stream_in, grad_middle, grad_normed)


def partner(block, distance):
    size = lax.axis_size("dp")
    return lax.ppermute(block, "dp", [(i, i ^ distance) for i in range(size)])


def across(block):
    return lax.ppermute(block, "section", [(0, 1), (1, 0)])


def halve(held, distance):
    bit = (lax.axis_index("dp") & distance) // distance
    half = held.shape[1] // 2
    mine = lax.dynamic_slice_in_dim(held, bit * half, half, 1)
    theirs = lax.dynamic_slice_in_dim(held, (1 - bit) * half, half, 1)
    return add_low(mine, partner(theirs, distance))


def add_low(left, right):
    return (left.astype(FULL) + right.astype(FULL)).astype(LOW)


def scatter(held, order):
    for distance in order:
        held = halve(held, distance)
    return held


def gather(shard, order):
    held = shard[None]
    for distance in reversed(order):
        held = jnp.concatenate([held, partner(held, distance)], axis=0)
    return held


def places(order):
    me = lax.axis_index("dp")
    count = len(order)
    numbers = []
    for entry in range(1 << count):
        other = 0
        for place, distance in enumerate(reversed(order)):
            if entry >> place & 1:
                other |= distance
        device = me ^ other
        number = jnp.int32(0)
        for place, distance in enumerate(order):
            number = number + ((device // distance) & 1) * (1 << (count - 1 - place))
        numbers.append(number)
    return jnp.stack(numbers).astype(jnp.int32)


def down_sum_kernel(place_ref, in_ref, out_ref):
    rows = out_ref.shape[2]
    for block in range(out_ref.shape[0]):
        out_ref[block, 0] = in_ref[0, block * rows : (block + 1) * rows, :].astype(FULL)


def down_sum(place, gathered, width):
    entries, held = gathered.shape[:2]
    rows = width // entries
    blocks = 2
    out = kernel_call(
        down_sum_kernel,
        "down_sum",
        pltpu.PrefetchScalarGridSpec(
            num_scalar_prefetch=1,
            grid=(entries,),
            in_specs=[pl.BlockSpec((1, held, width), lambda e, p: (e, 0, 0))],
            out_specs=pl.BlockSpec((blocks, 1, rows, width), lambda e, p: (0, p[e], 0, 0)),
        ),
        jax.ShapeDtypeStruct((blocks, entries, rows, width), FULL),
        0,
        6 * blocks * width * width,
    )(place, gathered)
    return out.reshape(blocks * width, width)


def first_sum_kernel(place_ref, a_ref, b_ref, out_ref):
    rows, columns = out_ref.shape[1:]
    width = columns // 4
    part = width // 3

    def block(number):
        if number < 3:
            return a_ref[0, number * rows : (number + 1) * rows, :].astype(FULL)
        return b_ref[0].astype(FULL)

    @pl.when(place_ref[0] == 0)
    def _():
        out_ref[0, :, 3 * width :] = block(0)
        for group in range(GROUPS):
            values = block(group + 1)
            for piece in range(3):
                column = own_column_static(group, piece, 0) * part
                out_ref[0, :, column : column + part] = values[:, piece * part : (piece + 1) * part]

    @pl.when(place_ref[0] == 1)
    def _():
        for group in range(4):
            out_ref[0, :, group * width : (group + 1) * width] = block(group)


def first_sum(place, a, b, width):
    entries = a.shape[0]
    rows = width // entries
    out = kernel_call(
        first_sum_kernel,
        "first_sum",
        pltpu.PrefetchScalarGridSpec(
            num_scalar_prefetch=1,
            grid=(entries,),
            in_specs=[
                pl.BlockSpec((1, 3 * rows, width), lambda e, p: (e, 0, 0)),
                pl.BlockSpec((1, rows, width), lambda e, p: (e, 0, 0)),
            ],
            out_specs=pl.BlockSpec((1, rows, 4 * width), lambda e, p: (p[e + 1], 0, 0)),
        ),
        jax.ShapeDtypeStruct((entries, rows, 4 * width), FULL),
        0,
        24 * width * width,
    )(place, a, b)
    return out.reshape(width, 4 * width)


def on_device(stream_in, cotangent, weights_first, down_weight, segments):
    rows_dev, length, compact_width = stream_in.shape
    width = compact_width + 1
    section = lax.axis_index("section").astype(jnp.int32)
    index = lax.axis_index("dp").astype(jnp.int32)
    size = lax.axis_size("dp")
    on_attention = section == 0
    where = jnp.stack([section, index & 3, index & 1])
    segments3 = segments.reshape(rows_dev, 1, length)
    bits = [1 << i for i in range(1, size.bit_length() - 1)]
    orders = ([1] + bits, [1] + bits[1:] + bits[:1])

    piece = weight_piece(where, weights_first)
    received = []
    for group in range(4):
        near = across(piece[group])
        beside = partner(near, 2)
        received.append((near, beside, partner(jnp.stack([near, beside]), 1)))

    nt, g = prep(where, stream_in, cotangent)
    ga = branch_grad(g, down_weight)
    attended = [attend(group, where, weights_first, received[group], nt, segments3) for group in range(GROUPS)]
    mixed = [a[1] for a in attended]
    middle, nm, nmt, sums_mid, out_weights = middle_of(
        where, weights_first, received[GROUPS], mixed, stream_in, segments3
    )
    (keep_dn, send_dn, keep_up, send_up, keep_out, send_out, grad_mid, gab, sums_out) = feed(
        where, weights_first, received, nm, nmt, g, ga, down_weight, middle, cotangent, segments3
    )
    received_out = across(send_out)

    dn = scatter(add_low(keep_dn, partner(send_dn, 1)), orders[0][1:])
    up = scatter(add_low(keep_up, partner(send_up, 1)), orders[1][1:])

    gm, delta, gw_out = mixed_grad(gab, out_weights, mixed)
    heads = HEADS // GROUPS
    grad_normed = None
    grads = []
    for group in range(GROUPS):
        qkv, _, total, w = attended[group]
        gw, grad_normed = attend_back(
            where, qkv, gm[group], total, delta[group * heads : (group + 1) * heads], segments3, w, nt, grad_normed
        )
        grads.append(gw)
    keep_grad, send_grad = input_grad(where, stream_in, grad_mid, grad_normed)
    received_grad = across(send_grad)

    rows = dn.shape[1]
    flat = lambda a: a.reshape(-1, width)
    scalars = (sums_mid + sums_out)[0, :3]

    def scalar_rows(values):
        high = values.astype(LOW)
        rest = values - high.astype(FULL)
        middle_part = rest.astype(LOW)
        low = (rest - middle_part.astype(FULL)).astype(LOW)
        packed = jnp.concatenate([high, middle_part, low])
        return jnp.zeros((16, width), LOW).at[0, :9].set(packed)

    def scalars_of(block):
        parts = block[..., 0, :9].astype(FULL)
        return parts[..., :3] + parts[..., 3:6] + parts[..., 6:9]

    lower, upper = flat(dn[:2]), flat(dn[2:])
    mine = jnp.concatenate([jnp.where(on_attention, lower, upper), flat(up)])
    theirs = jnp.concatenate([jnp.where(on_attention, upper, lower), flat(up), scalar_rows(scalars)])
    swapped = across(theirs)
    shard = add_low(mine, swapped[:-16])
    pair = scalars + scalars_of(swapped[-16:])
    dn_rows = 2 * rows

    attn_a = scatter(jnp.stack([gw_out] + grads[:2]), orders[1])
    attn_b = scatter(jnp.stack(grads[2:]), orders[1])
    attn = jnp.concatenate([flat(attn_a), flat(attn_b)])
    attn = add_low(attn, across(attn))
    first_a = jnp.where(on_attention, attn[: 3 * rows], shard[dn_rows : dn_rows + 3 * rows])
    first_b = jnp.where(on_attention, attn[3 * rows :], shard[dn_rows + 3 * rows :])
    down_all = gather(jnp.concatenate([shard[:dn_rows], scalar_rows(pair)]), orders[0])
    grad_down = down_sum(places(orders[0]), down_all, width)
    grad_first = first_sum(
        jnp.concatenate([section[None], places(orders[1])]), gather(first_a, orders[1]), gather(first_b, orders[1]), width
    )
    totals = jnp.sum(scalars_of(down_all[:, dn_rows:]), axis=0)
    square = jnp.where(on_attention, totals[0], totals[1])
    residual_rms = jnp.sqrt(square / (totals[2] * width)).reshape(1)
    slots = jnp.float32(rows_dev * length * size)
    token_count = jnp.where(on_attention, totals[2], slots - totals[2]).astype(jnp.int32).reshape(1)

    def stacked(kept, other):
        return jnp.where(on_attention, jnp.stack([kept, other]), jnp.stack([other, kept]))[None]

    return (
        stacked(keep_out, received_out),
        stacked(keep_grad, received_grad),
        grad_first[None],
        grad_down,
        residual_rms,
        token_count,
    )


def solution(mesh):
    placed = (
        P("dp", None, None),
        P("dp", None, None),
        P("section", None, None),
        P(),
        P("dp", None),
    )
    return jax.shard_map(
        on_device,
        mesh=mesh,
        in_specs=placed,
        out_specs=(
            P("section", "dp", None, None),
            P("section", "dp", None, None),
            P("section", None, None),
            P("section", None),
            P("section"),
            P("section"),
        ),
        check_vma=False,
    )
```

time: 1080 us -> 485 us (0.45)
  waiting for transfers between devices: 419 us -> 161 us
  matrix products: 251 us -> 0 us
  Pallas kernels: 0 us -> 178 us
  local copies, waits for them, and re-layouts: 184 us -> 57 us
  other arithmetic: 133 us -> 35.1 us
  blocking collectives: 34.1 us -> 0 us
  starting transfers between devices: 7.73 us -> 41.6 us
  loops' own time: 27.5 us -> 0 us
  between operations: 19.3 us -> 7.28 us
    psum x1 -> x0, waiting for transfers between devices: 331 us -> none  [on_device(): lax.psum((first_sum, down_sum, carried[7], carried[8]), 'dp')]
    dot_general x40 -> x0, matrix products: 251 us -> none  [the longest x4 50 us: attend_back(): jnp.einsum('qhd,khd->hqk', grad_block, values[:reach], preferred_element_...]
    pallas_call x0 -> x15, Pallas kernels: none -> 178 us  [the longest x3 42.3 us: attend_back(): kernel_call(body, 'attend_back', pltpu.PrefetchScalarGridSpec(num_scalar_...]
    ppermute x5 -> x44, waiting for transfers between devices: 88.6 us -> 161 us  [the longest x36 112 us: partner(): return lax.ppermute(block, 'dp', [(i, i ^ distance) for i in range(size)])]
    cond x121 -> x0, local copies, waits for them, and re-layouts: 53.4 us -> none
    slice x37 -> x3, local copies, waits for them, and re-layouts: 54.1 us -> 2.09 us  [the longest x1 1.47 us: on_device(): delta[group * heads:(group + 1) * heads]]
    convert_element_type x12 -> x22, other arithmetic: 56.9 us -> 11.5 us  [the longest x17 11.4 us: add_low(): return (left.astype(FULL) + right.astype(FULL)).astype(LOW)]
    another operation x9 -> x1, local copies, waits for them, and re-layouts: 42.9 us -> 0.68 us  [places(): return jnp.stack(numbers).astype(jnp.int32)]
  transfers between devices with their start and end apart: 6 -> 44, of which waited for: 4 -> 19; matrix products, arithmetic and copies ran while one was open for 23% -> 16% of each run, Pallas kernels for 0% -> 22%
where the time goes in v1:
time: 485 us; the launch traced here: 480 us
  Pallas kernels  178 us (37%)
  waiting for transfers between devices  161 us (33%)
  local copies, waits for them, and re-layouts  57 us (12%)
  starting transfers between devices  41.6 us (9%)
  other arithmetic  35.1 us (7%)
  between operations  7.28 us (2%)
    ppermute x36, waiting for transfers between devices, partner(): return lax.ppermute(block, 'dp', [(i, i ^ distance) for i in range(size)])  112 us
    ppermute x8, waiting for transfers between devices, across(): return lax.ppermute(block, 'section', [(0, 1), (1, 0)])  49.3 us
    unnamed x97, local copies, waits for them, and re-layouts  43.5 us
    pallas_call x3, Pallas kernels, attend_back(): kernel_call(body, 'attend_back', pltpu.PrefetchScalarGridSpec(num_scalar_...  42.3 us
    pallas_call x1, Pallas kernels, feed(): kernel_call(feed_kernel, 'feed', pltpu.PrefetchScalarGridSpec(num_scalar_...  42.1 us
    ppermute x36, starting transfers between devices, partner(): return lax.ppermute(block, 'dp', [(i, i ^ distance) for i in range(size)])  31.5 us
    pallas_call x3, Pallas kernels, attend(): kernel_call(functools.partial(attend_kernel, group), 'attend', pltpu.Pref...  26.7 us
    pallas_call x1, Pallas kernels, first_sum(): kernel_call(first_sum_kernel, 'first_sum', pltpu.PrefetchScalarGridSpec(n...  12.4 us
  transfers between devices with their start and end apart: 44, of which 19 were waited for; matrix products, arithmetic and copies ran while one was open for 16% of the time, Pallas kernels for 22%

profile of v1, /device:TPU:0, one launch (start us, length us, event | category | flops | bytes accessed | tf_op | source)
XLA Modules:
  0.0 480.1 jit_solution(9411361626997663713)
XLA Ops:
  1.3 8.1 %weight_piece.1 = bf16[4,192,768]{2,1,0:T(8,128)(2,1)} custom-call(s32[3]{0:T(128)} %pad_add_fusion.where_ref, bf16[1,768,3072]{2,1,0:T(8,128)(2,1)} %own_ref.9), custom_call_target="tpu_custom_call" | custom-call | bytes 2359296 | tf_op jit(solution)/shard_map/weight_piece/pallas_call | solution.py:152
  9.4 2.2 slice_bitcast_fusion
  11.6 3.0 collective-permute-start.6
  14.6 2.0 collective-permute-start
  16.6 5.9 %collective-permute-done.6.near_ref.refs_6_ = bf16[192,768]{1,0:T(8,128)(2,1)} collective-permute-done((bf16[192,768]{1,0:T(8,128)(2,1)S(1)}, bf16[192,768]{1,0:T(8,128)(2,1)}, u32[]{:S(2)}, u32[]{:S(2)}) %collective-permute-start.6) | collective-permute-done | bytes 294944 | tf_op jit(solution)/shard_map/ppermute | solution.py:685
  22.5 2.0 collective-permute-start.7
  24.5 6.8 %copy.11.x_ref.refs_3_ = bf16[2,1024,767]{2,1,0:T(8,128)(2,1)} copy(bf16[2,1024,767]{1,0,2:T(2,128)(2,1)S(1)} %copy-done.9) | data formatting | bytes 6283264 | tf_op args[0]
  31.3 8.8 %copy.12.cot_ref.refs_18_ = bf16[2,1024,767]{2,1,0:T(8,128)(2,1)} copy(bf16[2,1024,767]{1,0,2:T(2,128)(2,1)} %param.10) | data formatting | bytes 6283264 | tf_op args[1]
  40.1 5.5 %prep.1 = (bf16[768,1024]{1,0:T(8,128)(2,1)}, bf16[1024,768]{1,0:T(8,128)(2,1)}) custom-call(s32[3]{0:T(128)} %pad_add_fusion.where_ref, bf16[2,1024,767]{2,1,0:T(8,128)(2,1)} %copy.11.x_ref.refs_3_, bf16[2,1024,767]{2,1,0:T(8,128)(2,1)} %copy.12.cot_ref.refs_18_), custom_call_target="tpu_custom_call" | custom-call | bytes 6291456 | tf_op jit(solution)/shard_map/prep/pallas_call | solution.py:88
  45.6 2.0 collective-permute-start.1
  48.9 9.3 %branch_grad.1.refs_15_ = bf16[4,1024,768]{2,1,0:T(8,128)(2,1)} custom-call(bf16[1024,768]{1,0:T(8,128)(2,1)} %get-tuple-element.77.g_ref.refs_14_, bf16[3072,768]{1,0:T(8,128)(2,1)} %refs_16_.1), custom_call_target="tpu_custom_call" | custom-call | flops 4831838208 | bytes 7864320 | tf_op jit(solution)/shard_map/branch_grad/pallas_call | solution.py:116
  62.9 2.0 collective-permute-done.10.beside_ref.refs_10_
  65.9 8.7 %attend.5 = (bf16[768,1024]{1,0:T(8,128)(2,1)}, bf16[256,1024]{1,0:T(8,128)(2,1)}, f32[4,1024]{1,0:T(4,128)}, bf16[768,768]{1,0:T(8,128)(2,1)}) custom-call(s32[3]{0:T(128)} %pad_add_fusion.where_ref, bf16[1,768,3072]{2,1,0:T(8,128)(2,1)} %own_ref.9, bf16[192,768]{1,0:T(8,128)(2,1)} %collective-permute-done.6.near_ref.refs_6_, ...), custom_call_target="tpu_custom_call" | custom-call | flops 4499999744 | bytes 6291456 | tf_op jit(solution)/shard_map/attend/pallas_call | solution.py:289
  75.5 8.8 %attend.4 = (bf16[768,1024]{1,0:T(8,128)(2,1)}, bf16[256,1024]{1,0:T(8,128)(2,1)}, f32[4,1024]{1,0:T(4,128)}, bf16[768,768]{1,0:T(8,128)(2,1)}) custom-call(s32[3]{0:T(128)} %pad_add_fusion.where_ref, bf16[1,768,3072]{2,1,0:T(8,128)(2,1)} %own_ref.9, bf16[192,768]{1,0:T(8,128)(2,1)} %collective-permute-done.3.near_ref.refs_3_, bf16[192,768]{1,0:T(8,128)(2,1)} %copy-done.35, ...), custom_call_target="tpu_custom_call" | custom-call | flops 4499999744 | bytes 6291456 | tf_op jit(solution)/shard_map/attend/pallas_call | solution.py:289
  84.3 9.2 %attend.3 = (bf16[768,1024]{1,0:T(8,128)(2,1)}, bf16[256,1024]{1,0:T(8,128)(2,1)}, f32[4,1024]{1,0:T(4,128)}, bf16[768,768]{1,0:T(8,128)(2,1)}) custom-call(s32[3]{0:T(128)} %pad_add_fusion.where_ref, bf16[1,768,3072]{2,1,0:T(8,128)(2,1)} %own_ref.9, bf16[192,768]{1,0:T(8,128)(2,1)} %collective-permute-done.near_ref.refs_0_, bf16[192,768]{1,0:T(8,128)(2,1)} %copy-done.36, ...), custom_call_target="tpu_custom_call" | custom-call | flops 4499999744 | bytes 6291456 | tf_op jit(solution)/shard_map/attend/pallas_call | solution.py:289
  94.3 8.3 %middle.1 = (bf16[1024,767]{1,0:T(8,128)(2,1)}, bf16[1024,768]{1,0:T(8,128)(2,1)}, bf16[768,1024]{1,0:T(8,128)(2,1)}, f32[8,128]{1,0:T(8,128)}, bf16[768,768]{1,0:T(8,128)(2,1)}) custom-call(s32[3]{0:T(128)} %pad_add_fusion.where_ref, bf16[1,768,3072]{2,1,0:T(8,128)(2,1)} %own_ref.9, bf16[192,768]{1,0:T(8,128)(2,1)} %copy-done.31, ...), custom_call_target="tpu_custom_call" | custom-call | flops 1207959552 | bytes 9437184 | tf_op jit(solution)/shard_map/middle/pallas_call | solution.py:439
  102.6 42.1 %feed.1 = (bf16[4,384,768]{2,1,0:T(8,128)(2,1)}, bf16[4,384,768]{2,1,0:T(8,128)(2,1)}, bf16[4,384,768]{2,1,0:T(8,128)(2,1)}, bf16[4,384,768]{2,1,0:T(8,128)(2,1)...) custom-call(s32[3]{0:T(128)} %pad_add_fusion.where_ref, ...), custom_call_target="tpu_custom_call" | custom-call | flops 32000000000 | bytes 23592960 | tf_op jit(solution)/shard_map/feed/pallas_call | solution.py:564
  145.3 6.0 %mixed_grad.1 = (bf16[256,1024]{1,0:T(8,128)(2,1)}, bf16[256,1024]{1,0:T(8,128)(2,1)}, bf16[256,1024]{1,0:T(8,128)(2,1)}, f32[12,1024]{1,0:T(8,128)}, bf16[768,768]{1,0:T(8,128)(2,1)}) custom-call(bf16[1024,768]{1,0:T(8,128)(2,1)} %get-tuple-element.83.gab_ref, bf16[768,768]{1,0:T(8,128)(2,1)} %get-tuple-element.84.w_ref, ...), custom_call_target="tpu_custom_call" | custom-call | flops 2415919104 | bytes 6291456 | tf_op jit(solution)/shard_map/mixed_grad/pallas_call | solution.py:628
  152.7 13.2 %attend_back.3 = (bf16[768,768]{1,0:T(8,128)(2,1)}, f32[768,1024]{1,0:T(8,128)}) custom-call(s32[3]{0:T(128)} %pad_add_fusion.where_ref, bf16[768,1024]{1,0:T(8,128)(2,1)} %get-tuple-element.93.refs_0_, bf16[256,1024]{1,0:T(8,128)(2,1)} %get-tuple-element.94.refs_1_, f32[4,1024]{1,0:T(4,128)} %get-tuple-element.95.refs_2_, ...), custom_call_target="tpu_custom_call" | custom-call | flops 8999999488 | bytes 6291456 | tf_op jit(solution)/shard_map/attend_back/pallas_call | solution.py:387
  165.9 14.6 %attend_back.4 = (bf16[768,768]{1,0:T(8,128)(2,1)}, f32[768,1024]{1,0:T(8,128)}) custom-call(s32[3]{0:T(128)} %pad_add_fusion.where_ref, bf16[768,1024]{1,0:T(8,128)(2,1)} %get-tuple-element.89.refs_0_, bf16[256,1024]{1,0:T(8,128)(2,1)} %get-tuple-element.90.refs_1_, f32[4,1024]{1,0:T(4,128)} %get-tuple-element.91.refs_2_, ...), custom_call_target="tpu_custom_call" | custom-call | flops 8999999488 | bytes 6291456 | tf_op jit(solution)/shard_map/attend_back/pallas_call | solution.py:387
  180.5 14.5 %attend_back.5 = (bf16[768,768]{1,0:T(8,128)(2,1)}, f32[768,1024]{1,0:T(8,128)}) custom-call(s32[3]{0:T(128)} %pad_add_fusion.where_ref, bf16[768,1024]{1,0:T(8,128)(2,1)} %get-tuple-element.82.refs_0_, bf16[256,1024]{1,0:T(8,128)(2,1)} %get-tuple-element.85.refs_1_, f32[4,1024]{1,0:T(4,128)} %get-tuple-element.86.refs_2_, ...), custom_call_target="tpu_custom_call" | custom-call | flops 8999999488 | bytes 6291456 | tf_op jit(solution)/shard_map/attend_back/pallas_call | solution.py:387
  195.0 2.0 dynamic-slice_bitcast_fusion
  199.4 2.2 fusion
  201.6 1.7 constant_dynamic-slice_fusion.8
  203.3 1.6 collective-permute-start.19
  204.9 8.1 %collective-permute-done.19 = bf16[1,192,768]{2,1,0:T(8,128)(2,1)} collective-permute-done((bf16[1,192,768]{2,1,0:T(8,128)(2,1)}, bf16[1,192,768]{2,1,0:T(8,128)(2,1)}, u32[]{:S(2)}, u32[]{:S(2)}) %collective-permute-start.19) | collective-permute-done | bytes 294944 | tf_op jit(solution)/shard_map/ppermute | solution.py:681
  214.2 2.7 collective-permute-start.20
  216.8 6.9 %collective-permute-done.20 = bf16[1,96,768]{2,1,0:T(8,128)(2,1)S(1)} collective-permute-done((bf16[1,96,768]{2,1,0:T(8,128)(2,1)S(1)}, bf16[1,96,768]{2,1,0:T(8,128)(2,1)S(1)}, u32[]{:S(2)}, u32[]{:S(2)}) %collective-permute-start.20) | collective-permute-done | bytes 147488 | tf_op jit(solution)/shard_map/ppermute | solution.py:681
  223.8 2.0 add_convert_fusion.2
  226.7 2.2 add_convert_fusion.1
  230.6 2.2 add_convert_fusion
  234.3 14.3 %collective-permute-done.15 = bf16[3,192,768]{2,1,0:T(8,128)(2,1)S(1)} collective-permute-done((bf16[3,192,768]{2,1,0:T(8,128)(2,1)S(1)}, bf16[3,192,768]{2,1,0:T(8,128)(2,1)S(1)}, u32[]{:S(2)}, u32[]{:S(2)}) %collective-permute-start.15) | collective-permute-done | bytes 884768 | tf_op jit(solution)/shard_map/ppermute | solution.py:681
  248.9 2.0 collective-permute-start.16
  251.5 6.8 %collective-permute-done.21 = bf16[1,48,768]{2,1,0:T(8,128)(2,1)S(1)} collective-permute-done((bf16[1,48,768]{2,1,0:T(8,128)(2,1)S(1)}, bf16[1,48,768]{2,1,0:T(8,128)(2,1)S(1)}, u32[]{:S(2)}, u32[]{:S(2)}) %collective-permute-start.21) | collective-permute-done | bytes 73760 | tf_op jit(solution)/shard_map/ppermute | solution.py:681
  258.3 22.2 %collective-permute-done.16 = bf16[3,96,768]{2,1,0:T(8,128)(2,1)S(1)} collective-permute-done((bf16[3,96,768]{2,1,0:T(8,128)(2,1)S(1)}, bf16[3,96,768]{2,1,0:T(8,128)(2,1)S(1)}, u32[]{:S(2)}, u32[]{:S(2)}) %collective-permute-start.16) | collective-permute-done | bytes 442400 | tf_op jit(solution)/shard_map/ppermute | solution.py:681
  281.6 4.2 collective-permute-start.25
  287.3 1.5 collective-permute-start.22
  288.9 19.7 %collective-permute-done.25 = bf16[4,96,768]{2,1,0:T(8,128)(2,1)S(1)} collective-permute-done((bf16[4,96,768]{2,1,0:T(8,128)(2,1)S(1)}, bf16[4,96,768]{2,1,0:T(8,128)(2,1)S(1)}, u32[]{:S(2)}, u32[]{:S(2)}) %collective-permute-start.25) | collective-permute-done | bytes 589856 | tf_op jit(solution)/shard_map/ppermute | solution.py:681
  310.2 12.1 %collective-permute-done.29 = bf16[4,96,768]{2,1,0:T(8,128)(2,1)S(1)} collective-permute-done((bf16[4,96,768]{2,1,0:T(8,128)(2,1)S(1)}, bf16[4,96,768]{2,1,0:T(8,128)(2,1)S(1)}, u32[]{:S(2)}, u32[]{:S(2)}) %collective-permute-start.29) | collective-permute-done | bytes 589856 | tf_op jit(solution)/shard_map/ppermute | solution.py:681
  322.6 1.6 collective-permute-start.30
  324.1 2.5 collective-permute-done.26
  326.7 2.6 collective-permute-done.30
  329.5 1.5 collective-permute-start.31
  331.0 7.2 %input_grad.1 = (bf16[1024,767]{1,0:T(8,128)(2,1)}, bf16[1024,767]{1,0:T(8,128)(2,1)}) custom-call(s32[3]{0:T(128)} %pad_add_fusion.where_ref, bf16[2,1024,767]{2,1,0:T(8,128)(2,1)} %copy.11.x_ref.refs_3_, bf16[1024,767]{1,0:T(8,128)(2,1)} %get-tuple-element.81.gmid_ref, f32[768,1024]{1,0:T(8,128)} %get-tuple-element.99.gn_ref), custom_call_target="tpu_custom_call" | custom-call | bytes 9437184 | tf_op jit(solution)/shard_map/input_grad/pallas_call | solution.py:660
  344.3 2.8 collective-permute-done.40
  347.5 3.5 collective-permute-start.33
  351.0 24.7 %collective-permute-done.13 = bf16[1024,767]{1,0:T(8,128)(2,1)S(1)} collective-permute-done((bf16[1024,767]{1,0:T(8,128)(2,1)}, bf16[1024,767]{1,0:T(8,128)(2,1)S(1)}, u32[]{:S(2)}, u32[]{:S(2)}) %collective-permute-start.13) | collective-permute-done | bytes 1570848 | tf_op jit(solution)/shard_map/ppermute | solution.py:685
  376.8 3.4 maximum_select_fusion.1
  380.3 1.7 constant_dynamic-update-slice_fusion.9
  386.9 18.7 %collective-permute-done.12 = bf16[1024,767]{1,0:T(8,128)(2,1)} collective-permute-done((bf16[1024,767]{1,0:T(8,128)(2,1)}, bf16[1024,767]{1,0:T(8,128)(2,1)}, u32[]{:S(2)}, u32[]{:S(2)}) %collective-permute-start.12) | collective-permute-done | bytes 1570848 | tf_op jit(solution)/shard_map/ppermute | solution.py:685
  405.6 3.7 maximum_select_fusion
  409.4 5.8 %copy.17 = bf16[1,2,1024,767]{2,1,3,0:T(2,128)(2,1)} copy(bf16[1,2,1024,767]{3,2,1,0:T(8,128)(2,1)S(1)} %maximum_select_fusion.1) | data formatting | bytes 6283264
  415.1 8.8 %copy.16 = bf16[1,2,1024,767]{2,1,3,0:T(2,128)(2,1)} copy(bf16[1,2,1024,767]{3,2,1,0:T(8,128)(2,1)} %maximum_select_fusion) | data formatting | bytes 6283264
  425.0 1.6 constant_dynamic-update-slice_fusion.8
  426.6 5.3 %collective-permute-done.37 = bf16[2,48,768]{2,1,0:T(8,128)(2,1)S(1)} collective-permute-done((bf16[2,48,768]{2,1,0:T(8,128)(2,1)S(1)}, bf16[2,48,768]{2,1,0:T(8,128)(2,1)S(1)}, u32[]{:S(2)}, u32[]{:S(2)}) %collective-permute-start.37) | collective-permute-done | bytes 147488 | tf_op jit(solution)/shard_map/ppermute | solution.py:681
  434.4 2.7 pad_maximum_fusion.1
  437.6 2.1 collective-permute-done.38
  440.9 1.8 collective-permute-done.39
  442.8 1.6 constant_dynamic-update-slice_fusion.11
  445.7 1.5 copy-done.10
  451.2 10.7 %down_sum.1 = f32[2,16,48,768]{3,2,1,0:T(8,128)} custom-call(s32[16]{0:T(128)} %stack.248.place_ref, bf16[16,112,768]{2,1,0:T(8,128)(2,1)} %copy-done.10), custom_call_target="tpu_custom_call" | custom-call | bytes 7077888 | tf_op jit(solution)/shard_map/down_sum/pallas_call | solution.py:740
  461.9 1.6 constant_dynamic-update-slice_fusion.a_ref
  463.5 1.8 copy-done.1
  465.3 12.4 %first_sum.1 = f32[16,48,3072]{2,1,0:T(8,128)} custom-call(s32[17]{0:T(128)} %concatenate.98.place_ref, bf16[16,144,768]{2,1,0:T(8,128)(2,1)} %copy-done.1, bf16[16,48,768]{2,1,0:T(8,128)(2,1)} %copy-done.25), custom_call_target="tpu_custom_call" | custom-call | bytes 14155776 | tf_op jit(solution)/shard_map/first_sum/pallas_call | solution.py:784
  (212 shorter events, 44.0 us)
Async XLA Ops:
  1.3 23.2 %copy-start.9 = (bf16[2,1024,767]{1,0,2:T(2,128)(2,1)S(1)}, bf16[2,1024,767]{1,0,2:T(2,128)(2,1)}, u32[]{:S(2)}) copy-start(bf16[2,1024,767]{1,0,2:T(2,128)(2,1)} %param.9) | copy-start | bytes 9424900
  11.6 10.9 %collective-permute-start.6 = (bf16[192,768]{1,0:T(8,128)(2,1)S(1)}, bf16[192,768]{1,0:T(8,128)(2,1)}, u32[]{:S(2)}, u32[]{:S(2)}) collective-permute-start(bf16[192,768]{1,0:T(8,128)(2,1)S(1)} %get-tuple-element.125), channel_id=1, source_target_pairs={{0,16},{16,0},{1,17},{17,1},{2,18},{18,2},{3,19},{19,3},{4,20},{20... | collective-permute-start | bytes 884744 | tf_op jit(solution)/shard_map/ppermute | solution.py:685
  14.5 31.0 %collective-permute-start.3 = (bf16[192,768]{1,0:T(8,128)(2,1)}, bf16[192,768]{1,0:T(8,128)(2,1)}, u32[]{:S(2)}, u32[]{:S(2)}) collective-permute-start(bf16[192,768]{1,0:T(8,128)(2,1)} %get-tuple-element.126), channel_id=1, source_target_pairs={{0,16},{16,0},{1,17},{17,1},{2,18},{18,2},{3,19},{19,3},{4,20},{20... | collective-permute-start | bytes 884744 | tf_op jit(solution)/shard_map/ppermute | solution.py:685
  14.6 31.0 %collective-permute-start = (bf16[192,768]{1,0:T(8,128)(2,1)}, bf16[192,768]{1,0:T(8,128)(2,1)}, u32[]{:S(2)}, u32[]{:S(2)}) collective-permute-start(bf16[192,768]{1,0:T(8,128)(2,1)} %get-tuple-element.127), channel_id=1, source_target_pairs={{0,16},{16,0},{1,17},{17,1},{2,18},{18,2},{3,19},{19,3},{4,20},{20... | collective-permute-start | bytes 884744 | tf_op jit(solution)/shard_map/ppermute | solution.py:685
  16.6 31.0 %collective-permute-start.9 = (bf16[192,768]{1,0:T(8,128)(2,1)}, bf16[192,768]{1,0:T(8,128)(2,1)S(1)}, u32[]{:S(2)}, u32[]{:S(2)}) collective-permute-start(bf16[192,768]{1,0:T(8,128)(2,1)} %get-tuple-element.124), channel_id=1, source_target_pairs={{0,16},{16,0},{1,17},{17,1},{2,18},{18,2},{3,19},{19,3},{4,20},{20... | collective-permute-start | bytes 884744 | tf_op jit(solution)/shard_map/ppermute | solution.py:685
  22.5 25.2 %collective-permute-start.7 = (bf16[192,768]{1,0:T(8,128)(2,1)}, bf16[192,768]{1,0:T(8,128)(2,1)}, u32[]{:S(2)}, u32[]{:S(2)}) collective-permute-start(bf16[192,768]{1,0:T(8,128)(2,1)} %collective-permute-done.6.near_ref.refs_6_), channel_id=1, source_target_pairs={{0,2},{1,3},{2,0},{3,1},{4,6},{5,7},{6,4},{7,5},{8,10},{9,11},{10,... | collective-permute-start | bytes 884744 | tf_op jit(solution)/shard_map/ppermute | solution.py:681
  45.6 13.3 %collective-permute-start.4 = (bf16[192,768]{1,0:T(8,128)(2,1)}, bf16[192,768]{1,0:T(8,128)(2,1)S(1)}, u32[]{:S(2)}, u32[]{:S(2)}) collective-permute-start(bf16[192,768]{1,0:T(8,128)(2,1)} %collective-permute-done.3.near_ref.refs_3_), channel_id=1, source_target_pairs={{0,2},{1,3},{2,0},{3,1},{4,6},{5,7},{6,4},{7,5},{8,10},{9,11},{10,... | collective-permute-start | bytes 884744 | tf_op jit(solution)/shard_map/ppermute | solution.py:681
  45.6 16.1 %collective-permute-start.1 = (bf16[192,768]{1,0:T(8,128)(2,1)}, bf16[192,768]{1,0:T(8,128)(2,1)S(1)}, u32[]{:S(2)}, u32[]{:S(2)}) collective-permute-start(bf16[192,768]{1,0:T(8,128)(2,1)} %collective-permute-done.near_ref.refs_0_), channel_id=1, source_target_pairs={{0,2},{1,3},{2,0},{3,1},{4,6},{5,7},{6,4},{7,5},{8,10},{9,11},{10,... | collective-permute-start | bytes 884744 | tf_op jit(solution)/shard_map/ppermute | solution.py:681
  47.6 17.3 %copy-start.31 = (bf16[192,768]{1,0:T(8,128)(2,1)}, bf16[192,768]{1,0:T(8,128)(2,1)S(1)}, u32[]{:S(2)}) copy-start(bf16[192,768]{1,0:T(8,128)(2,1)S(1)} %collective-permute-done.9.near_ref.refs_9_) | copy-start | bytes 884740
  47.6 17.3 %collective-permute-start.10 = (bf16[192,768]{1,0:T(8,128)(2,1)S(1)}, bf16[192,768]{1,0:T(8,128)(2,1)S(1)}, u32[]{:S(2)}, u32[]{:S(2)}) collective-permute-start(bf16[192,768]{1,0:T(8,128)(2,1)S(1)} %collective-permute-done.9.near_ref.refs_9_), channel_id=1, source_target_pairs={{0,2},{1,3},{2,0},{3,1},{4,6},{5,7},{6,4},{7,5},{8,10},{9,11},{10,... | collective-permute-start | bytes 884744 | tf_op jit(solution)/shard_map/ppermute | solution.py:681
  48.9 16.2 %collective-permute-start.8 = (bf16[2,192,768]{2,1,0:T(8,128)(2,1)S(1)}, bf16[2,192,768]{2,1,0:T(8,128)(2,1)S(1)}, u32[]{:S(2)}, u32[]{:S(2)}) collective-permute-start(bf16[2,192,768]{2,1,0:T(8,128)(2,1)S(1)} %pad_maximum_fusion.7), channel_id=1, source_target_pairs={{0,1},{1,0},{2,3},{3,2},{4,5},{5,4},{6,7},{7,6},{8,9},{9,8},{10,11... | collective-permute-start | bytes 1769480 | tf_op jit(solution)/shard_map/ppermute | solution.py:681
  48.9 9.3 %copy-start.37 = (s32[2,1024]{1,0:T(2,128)S(1)}, s32[2,1024]{1,0:T(2,128)}, u32[]{:S(2)}) copy-start(s32[2,1024]{1,0:T(2,128)} %param.13) | copy-start | bytes 24580
  60.0 14.7 %collective-permute-start.5 = (bf16[2,192,768]{2,1,0:T(8,128)(2,1)S(1)}, bf16[2,192,768]{2,1,0:T(8,128)(2,1)S(1)}, u32[]{:S(2)}, u32[]{:S(2)}) collective-permute-start(bf16[2,192,768]{2,1,0:T(8,128)(2,1)S(1)} %pad_maximum_fusion.6), channel_id=1, source_target_pairs={{0,1},{1,0},{2,3},{3,2},{4,5},{5,4},{6,7},{7,6},{8,9},{9,8},{10,11... | collective-permute-start | bytes 1769480 | tf_op jit(solution)/shard_map/ppermute | solution.py:681
  61.7 13.0 %copy-start.36 = (bf16[192,768]{1,0:T(8,128)(2,1)}, bf16[192,768]{1,0:T(8,128)(2,1)S(1)}, u32[]{:S(2)}) copy-start(bf16[192,768]{1,0:T(8,128)(2,1)S(1)} %collective-permute-done.1.beside_ref.refs_1_) | copy-start | bytes 884740
  62.9 21.5 %collective-permute-start.2 = (bf16[2,192,768]{2,1,0:T(8,128)(2,1)S(1)}, bf16[2,192,768]{2,1,0:T(8,128)(2,1)}, u32[]{:S(2)}, u32[]{:S(2)}) collective-permute-start(bf16[2,192,768]{2,1,0:T(8,128)(2,1)S(1)} %pad_maximum_fusion.5), channel_id=1, source_target_pairs={{0,1},{1,0},{2,3},{3,2},{4,5},{5,4},{6,7},{7,6},{8,9},{9,8},{10,11... | collective-permute-start | bytes 1769480 | tf_op jit(solution)/shard_map/ppermute | solution.py:681
  64.9 9.8 %copy-start.32 = (bf16[192,768]{1,0:T(8,128)(2,1)}, bf16[192,768]{1,0:T(8,128)(2,1)S(1)}, u32[]{:S(2)}) copy-start(bf16[192,768]{1,0:T(8,128)(2,1)S(1)} %collective-permute-done.10.beside_ref.refs_10_) | copy-start | bytes 884740
  65.0 28.6 %collective-permute-start.11 = (bf16[2,192,768]{2,1,0:T(8,128)(2,1)S(1)}, bf16[2,192,768]{2,1,0:T(8,128)(2,1)S(1)}, u32[]{:S(2)}, u32[]{:S(2)}) collective-permute-start(bf16[2,192,768]{2,1,0:T(8,128)(2,1)S(1)} %pad_maximum_fusion.8), channel_id=1, source_target_pairs={{0,1},{1,0},{2,3},{3,2},{4,5},{5,4},{6,7},{7,6},{8,9},{9,8},{10,11... | collective-permute-start | bytes 1769480 | tf_op jit(solution)/shard_map/ppermute | solution.py:681
  144.8 81.9 %collective-permute-start.23 = (bf16[4,384,768]{2,1,0:T(8,128)(2,1)}, bf16[4,384,768]{2,1,0:T(8,128)(2,1)}, u32[]{:S(2)}, u32[]{:S(2)}) collective-permute-start(bf16[4,384,768]{2,1,0:T(8,128)(2,1)} %get-tuple-element.107), channel_id=1, source_target_pairs={{0,1},{1,0},{2,3},{3,2},{4,5},{5,4},{6,7},{7,6},{8,9},{9,8},{10,11... | collective-permute-start | bytes 7077896 | tf_op jit(solution)/shard_map/ppermute | solution.py:681
  180.5 16.5 %copy-start.29 = (bf16[768,768]{1,0:T(8,128)(2,1)S(1)}, bf16[768,768]{1,0:T(8,128)(2,1)}, u32[]{:S(2)}) copy-start(bf16[768,768]{1,0:T(8,128)(2,1)} %get-tuple-element.103) | copy-start | bytes 3538948
  180.5 16.5 %copy-start.30 = (bf16[768,768]{1,0:T(8,128)(2,1)S(1)}, bf16[768,768]{1,0:T(8,128)(2,1)}, u32[]{:S(2)}) copy-start(bf16[768,768]{1,0:T(8,128)(2,1)} %get-tuple-element.104) | copy-start | bytes 3538948
  197.0 2.4 collective-permute-start.18
  198.9 24.9 %collective-permute-start.14 = (bf16[3,384,768]{2,1,0:T(8,128)(2,1)}, bf16[3,384,768]{2,1,0:T(8,128)(2,1)}, u32[]{:S(2)}, u32[]{:S(2)}) collective-permute-start(bf16[3,384,768]{2,1,0:T(8,128)(2,1)} %constant_dynamic-slice_fusion.12), channel_id=1, source_target_pairs={{0,1},{1,0},{2,3},{3,2},{4,5},{5,4},{6,7},{7,6},{8,9},{9,8},{10,11... | collective-permute-start | bytes 5308424 | tf_op jit(solution)/shard_map/ppermute | solution.py:681
  199.4 30.2 %collective-permute-start.27 = (bf16[4,384,768]{2,1,0:T(8,128)(2,1)}, bf16[4,384,768]{2,1,0:T(8,128)(2,1)}, u32[]{:S(2)}, u32[]{:S(2)}) collective-permute-start(bf16[4,384,768]{2,1,0:T(8,128)(2,1)} %get-tuple-element.109), channel_id=1, source_target_pairs={{0,1},{1,0},{2,3},{3,2},{4,5},{5,4},{6,7},{7,6},{8,9},{9,8},{10,11... | collective-permute-start | bytes 7077896 | tf_op jit(solution)/shard_map/ppermute | solution.py:681
  203.3 9.7 %collective-permute-start.19 = (bf16[1,192,768]{2,1,0:T(8,128)(2,1)}, bf16[1,192,768]{2,1,0:T(8,128)(2,1)}, u32[]{:S(2)}, u32[]{:S(2)}) collective-permute-start(bf16[1,192,768]{2,1,0:T(8,128)(2,1)} %constant_dynamic-slice_fusion.8), channel_id=1, source_target_pairs={{0,4},{1,5},{2,6},{3,7},{4,0},{5,1},{6,2},{7,3},{8,12},{9,13},{10,... | collective-permute-start | bytes 884744 | tf_op jit(solution)/shard_map/ppermute | solution.py:681
  214.2 9.6 %collective-permute-start.20 = (bf16[1,96,768]{2,1,0:T(8,128)(2,1)S(1)}, bf16[1,96,768]{2,1,0:T(8,128)(2,1)S(1)}, u32[]{:S(2)}, u32[]{:S(2)}) collective-permute-start(bf16[1,96,768]{2,1,0:T(8,128)(2,1)S(1)} %constant_dynamic-slice_fusion.7), channel_id=1, source_target_pairs={{0,8},{1,9},{2,10},{3,11},{4,12},{5,13},{6,14},{7,15},{8,0},{9,1},... | collective-permute-start | bytes 442376 | tf_op jit(solution)/shard_map/ppermute | solution.py:681
  225.9 22.7 %collective-permute-start.15 = (bf16[3,192,768]{2,1,0:T(8,128)(2,1)S(1)}, bf16[3,192,768]{2,1,0:T(8,128)(2,1)S(1)}, u32[]{:S(2)}, u32[]{:S(2)}) collective-permute-start(bf16[3,192,768]{2,1,0:T(8,128)(2,1)S(1)} %constant_dynamic-slice_fusion.11), channel_id=1, source_target_pairs={{0,4},{1,5},{2,6},{3,7},{4,0},{5,1},{6,2},{7,3},{8,12},{9,13},{10,... | collective-permute-start | bytes 2654216 | tf_op jit(solution)/shard_map/ppermute | solution.py:681
  229.0 52.3 %collective-permute-start.24 = (bf16[4,192,768]{2,1,0:T(8,128)(2,1)S(1)}, bf16[4,192,768]{2,1,0:T(8,128)(2,1)S(1)}, u32[]{:S(2)}, u32[]{:S(2)}) collective-permute-start(bf16[4,192,768]{2,1,0:T(8,128)(2,1)S(1)} %constant_dynamic-slice_fusion.5), channel_id=1, source_target_pairs={{0,2},{1,3},{2,0},{3,1},{4,6},{5,7},{6,4},{7,5},{8,10},{9,11},{10,... | collective-permute-start | bytes 3538952 | tf_op jit(solution)/shard_map/ppermute | solution.py:681
  232.9 52.9 %collective-permute-start.28 = (bf16[4,192,768]{2,1,0:T(8,128)(2,1)S(1)}, bf16[4,192,768]{2,1,0:T(8,128)(2,1)S(1)}, u32[]{:S(2)}, u32[]{:S(2)}) collective-permute-start(bf16[4,192,768]{2,1,0:T(8,128)(2,1)S(1)} %constant_dynamic-slice_fusion.2), channel_id=1, source_target_pairs={{0,4},{1,5},{2,6},{3,7},{4,0},{5,1},{6,2},{7,3},{8,12},{9,13},{10,... | collective-permute-start | bytes 3538952 | tf_op jit(solution)/shard_map/ppermute | solution.py:681
  248.9 31.7 %collective-permute-start.16 = (bf16[3,96,768]{2,1,0:T(8,128)(2,1)S(1)}, bf16[3,96,768]{2,1,0:T(8,128)(2,1)S(1)}, u32[]{:S(2)}, u32[]{:S(2)}) collective-permute-start(bf16[3,96,768]{2,1,0:T(8,128)(2,1)S(1)} %constant_dynamic-slice_fusion.10), channel_id=1, source_target_pairs={{0,8},{1,9},{2,10},{3,11},{4,12},{5,13},{6,14},{7,15},{8,0},{9,1},... | collective-permute-start | bytes 1327112 | tf_op jit(solution)/shard_map/ppermute | solution.py:681
  250.8 7.4 %collective-permute-start.21 = (bf16[1,48,768]{2,1,0:T(8,128)(2,1)S(1)}, bf16[1,48,768]{2,1,0:T(8,128)(2,1)S(1)}, u32[]{:S(2)}, u32[]{:S(2)}) collective-permute-start(bf16[1,48,768]{2,1,0:T(8,128)(2,1)S(1)} %constant_dynamic-slice_fusion.6), channel_id=1, source_target_pairs={{0,2},{1,3},{2,0},{3,1},{4,6},{5,7},{6,4},{7,5},{8,10},{9,11},{10,... | collective-permute-start | bytes 221192 | tf_op jit(solution)/shard_map/ppermute | solution.py:681
  280.7 6.6 %collective-permute-start.17 = (bf16[3,48,768]{2,1,0:T(8,128)(2,1)S(1)}, bf16[3,48,768]{2,1,0:T(8,128)(2,1)S(1)}, u32[]{:S(2)}, u32[]{:S(2)}) collective-permute-start(bf16[3,48,768]{2,1,0:T(8,128)(2,1)S(1)} %constant_dynamic-slice_fusion.9), channel_id=1, source_target_pairs={{0,2},{1,3},{2,0},{3,1},{4,6},{5,7},{6,4},{7,5},{8,10},{9,11},{10,... | collective-permute-start | bytes 663560 | tf_op jit(solution)/shard_map/ppermute | solution.py:681
  281.6 26.9 %collective-permute-start.25 = (bf16[4,96,768]{2,1,0:T(8,128)(2,1)S(1)}, bf16[4,96,768]{2,1,0:T(8,128)(2,1)S(1)}, u32[]{:S(2)}, u32[]{:S(2)}) collective-permute-start(bf16[4,96,768]{2,1,0:T(8,128)(2,1)S(1)} %constant_dynamic-slice_fusion.4), channel_id=1, source_target_pairs={{0,4},{1,5},{2,6},{3,7},{4,0},{5,1},{6,2},{7,3},{8,12},{9,13},{10,... | collective-permute-start | bytes 1769480 | tf_op jit(solution)/shard_map/ppermute | solution.py:681
  286.2 36.2 %collective-permute-start.29 = (bf16[4,96,768]{2,1,0:T(8,128)(2,1)S(1)}, bf16[4,96,768]{2,1,0:T(8,128)(2,1)S(1)}, u32[]{:S(2)}, u32[]{:S(2)}) collective-permute-start(bf16[4,96,768]{2,1,0:T(8,128)(2,1)S(1)} %constant_dynamic-slice_fusion.1), channel_id=1, source_target_pairs={{0,8},{1,9},{2,10},{3,11},{4,12},{5,13},{6,14},{7,15},{8,0},{9,1},... | collective-permute-start | bytes 1769480 | tf_op jit(solution)/shard_map/ppermute | solution.py:681
  287.3 52.8 %collective-permute-start.22 = (bf16[192,768]{1,0:T(8,128)(2,1)S(1)}, bf16[192,768]{1,0:T(8,128)(2,1)S(1)}, u32[]{:S(2)}, u32[]{:S(2)}) collective-permute-start(bf16[192,768]{1,0:T(8,128)(2,1)S(1)} %pad_maximum_fusion.12), channel_id=1, source_target_pairs={{0,16},{16,0},{1,17},{17,1},{2,18},{18,2},{3,19},{19,3},{4,20},{20... | collective-permute-start | bytes 884744 | tf_op jit(solution)/shard_map/ppermute | solution.py:685
  308.8 17.9 %collective-permute-start.26 = (bf16[4,48,768]{2,1,0:T(8,128)(2,1)S(1)}, bf16[4,48,768]{2,1,0:T(8,128)(2,1)S(1)}, u32[]{:S(2)}, u32[]{:S(2)}) collective-permute-start(bf16[4,48,768]{2,1,0:T(8,128)(2,1)S(1)} %constant_dynamic-slice_fusion.3), channel_id=1, source_target_pairs={{0,8},{1,9},{2,10},{3,11},{4,12},{5,13},{6,14},{7,15},{8,0},{9,1},... | collective-permute-start | bytes 884744 | tf_op jit(solution)/shard_map/ppermute | solution.py:681
  322.6 6.8 %collective-permute-start.30 = (bf16[4,48,768]{2,1,0:T(8,128)(2,1)S(1)}, bf16[4,48,768]{2,1,0:T(8,128)(2,1)S(1)}, u32[]{:S(2)}, u32[]{:S(2)}) collective-permute-start(bf16[4,48,768]{2,1,0:T(8,128)(2,1)S(1)} %constant_dynamic-slice_fusion), channel_id=1, source_target_pairs={{0,2},{1,3},{2,0},{3,1},{4,6},{5,7},{6,4},{7,5},{8,10},{9,11},{10,... | collective-permute-start | bytes 884744 | tf_op jit(solution)/shard_map/ppermute | solution.py:681
  329.5 10.8 %collective-permute-start.31 = (bf16[304,768]{1,0:T(8,128)(2,1)S(1)}, bf16[304,768]{1,0:T(8,128)(2,1)S(1)}, u32[]{:S(2)}, u32[]{:S(2)}) collective-permute-start(bf16[304,768]{1,0:T(8,128)(2,1)S(1)} %fusion.2), channel_id=1, source_target_pairs={{0,16},{16,0},{1,17},{17,1},{2,18},{18,2},{3,19},{19,3},{4,20},{20... | collective-permute-start | bytes 1400840 | tf_op jit(solution)/shard_map/ppermute | solution.py:685
  338.2 37.5 %collective-permute-start.13 = (bf16[1024,767]{1,0:T(8,128)(2,1)}, bf16[1024,767]{1,0:T(8,128)(2,1)S(1)}, u32[]{:S(2)}, u32[]{:S(2)}) collective-permute-start(bf16[1024,767]{1,0:T(8,128)(2,1)} %get-tuple-element.101), channel_id=1, source_target_pairs={{0,16},{16,0},{1,17},{17,1},{2,18},{18,2},{3,19},{19,3},{4,20},{20... | collective-permute-start | bytes 4712456 | tf_op jit(solution)/shard_map/ppermute | solution.py:685
  338.7 66.9 %collective-permute-start.12 = (bf16[1024,767]{1,0:T(8,128)(2,1)}, bf16[1024,767]{1,0:T(8,128)(2,1)}, u32[]{:S(2)}, u32[]{:S(2)}) collective-permute-start(bf16[1024,767]{1,0:T(8,128)(2,1)} %get-tuple-element.80), channel_id=1, source_target_pairs={{0,16},{16,0},{1,17},{17,1},{2,18},{18,2},{3,19},{19,3},{4,20},{20... | collective-permute-start | bytes 4712456 | tf_op jit(solution)/shard_map/ppermute | solution.py:685
  340.6 6.9 %copy-start.16 = (bf16[1,112,768]{2,1,0:T(8,128)(2,1)}, bf16[1,112,768]{2,1,0:T(8,128)(2,1)S(1)}, u32[]{:S(2)}) copy-start(bf16[1,112,768]{2,1,0:T(8,128)(2,1)S(1)} %fusion.6) | copy-start | bytes 516100
  340.6 6.5 %collective-permute-start.40 = (bf16[1,112,768]{2,1,0:T(8,128)(2,1)S(1)}, bf16[1,112,768]{2,1,0:T(8,128)(2,1)S(1)}, u32[]{:S(2)}, u32[]{:S(2)}) collective-permute-start(bf16[1,112,768]{2,1,0:T(8,128)(2,1)S(1)} %fusion.6), channel_id=1, source_target_pairs={{0,8},{1,9},{2,10},{3,11},{4,12},{5,13},{6,14},{7,15},{8,0},{9,1},... | collective-permute-start | bytes 516104 | tf_op jit(solution)/shard_map/ppermute | solution.py:681
  341.5 34.2 %copy-start.6 = (bf16[1,144,768]{2,1,0:T(8,128)(2,1)}, bf16[1,144,768]{2,1,0:T(8,128)(2,1)S(1)}, u32[]{:S(2)}) copy-start(bf16[1,144,768]{2,1,0:T(8,128)(2,1)S(1)} %get-tuple-element.123) | copy-start | bytes 663556
  341.5 6.0 %collective-permute-start.32 = (bf16[1,144,768]{2,1,0:T(8,128)(2,1)S(1)}, bf16[1,144,768]{2,1,0:T(8,128)(2,1)S(1)}, u32[]{:S(2)}, u32[]{:S(2)}) collective-permute-start(bf16[1,144,768]{2,1,0:T(8,128)(2,1)S(1)} %get-tuple-element.123), channel_id=1, source_target_pairs={{0,2},{1,3},{2,0},{3,1},{4,6},{5,7},{6,4},{7,5},{8,10},{9,11},{10,... | collective-permute-start | bytes 663560 | tf_op jit(solution)/shard_map/ppermute | solution.py:681
  347.1 85.8 %copy-start.14 = (bf16[1,112,768]{2,1,0:T(8,128)(2,1)}, bf16[1,112,768]{2,1,0:T(8,128)(2,1)S(1)}, u32[]{:S(2)}) copy-start(bf16[1,112,768]{2,1,0:T(8,128)(2,1)S(1)} %collective-permute-done.40) | copy-start | bytes 516100
  347.2 36.4 %collective-permute-start.41 = (bf16[2,112,768]{2,1,0:T(8,128)(2,1)S(1)}, bf16[2,112,768]{2,1,0:T(8,128)(2,1)S(1)}, u32[]{:S(2)}, u32[]{:S(2)}) collective-permute-start(bf16[2,112,768]{2,1,0:T(8,128)(2,1)S(1)} %pad_maximum_fusion.11), channel_id=1, source_target_pairs={{0,4},{1,5},{2,6},{3,7},{4,0},{5,1},{6,2},{7,3},{8,12},{9,13},{10,... | collective-permute-start | bytes 1032200 | tf_op jit(solution)/shard_map/ppermute | solution.py:681
  347.5 37.6 %copy-start.4 = (bf16[1,144,768]{2,1,0:T(8,128)(2,1)}, bf16[1,144,768]{2,1,0:T(8,128)(2,1)S(1)}, u32[]{:S(2)}) copy-start(bf16[1,144,768]{2,1,0:T(8,128)(2,1)S(1)} %collective-permute-done.32) | copy-start | bytes 663556
  347.5 37.6 %collective-permute-start.33 = (bf16[2,144,768]{2,1,0:T(8,128)(2,1)S(1)}, bf16[2,144,768]{2,1,0:T(8,128)(2,1)S(1)}, u32[]{:S(2)}, u32[]{:S(2)}) collective-permute-start(bf16[2,144,768]{2,1,0:T(8,128)(2,1)S(1)} %pad_maximum_fusion.10), channel_id=1, source_target_pairs={{0,8},{1,9},{2,10},{3,11},{4,12},{5,13},{6,14},{7,15},{8,0},{9,1},... | collective-permute-start | bytes 1327112 | tf_op jit(solution)/shard_map/ppermute | solution.py:681
  376.8 6.7 %copy-start.17 = (bf16[1,112,768]{2,1,0:T(8,128)(2,1)S(1)}, bf16[1,112,768]{2,1,0:T(8,128)(2,1)}, u32[]{:S(2)}) copy-start(bf16[1,112,768]{2,1,0:T(8,128)(2,1)} %copy-done.16) | copy-start | bytes 516100
  380.3 25.3 %copy-start.22 = (bf16[1024,767]{1,0:T(8,128)(2,1)S(1)}, bf16[1024,767]{1,0:T(8,128)(2,1)}, u32[]{:S(2)}) copy-start(bf16[1024,767]{1,0:T(8,128)(2,1)} %get-tuple-element.79) | copy-start | bytes 4712452
  382.1 41.9 %collective-permute-start.36 = (bf16[1,48,768]{2,1,0:T(8,128)(2,1)}, bf16[1,48,768]{2,1,0:T(8,128)(2,1)}, u32[]{:S(2)}, u32[]{:S(2)}) collective-permute-start(bf16[1,48,768]{2,1,0:T(8,128)(2,1)} %get-tuple-element.121), channel_id=1, source_target_pairs={{0,2},{1,3},{2,0},{3,1},{4,6},{5,7},{6,4},{7,5},{8,10},{9,11},{10,... | collective-permute-start | bytes 221192 | tf_op jit(solution)/shard_map/ppermute | solution.py:681
  384.5 48.4 %collective-permute-start.42 = (bf16[4,112,768]{2,1,0:T(8,128)(2,1)}, bf16[4,112,768]{2,1,0:T(8,128)(2,1)}, u32[]{:S(2)}, u32[]{:S(2)}) collective-permute-start(bf16[4,112,768]{2,1,0:T(8,128)(2,1)} %pad_maximum_fusion.4), channel_id=1, source_target_pairs={{0,2},{1,3},{2,0},{3,1},{4,6},{5,7},{6,4},{7,5},{8,10},{9,11},{10,... | collective-permute-start | bytes 2064392 | tf_op jit(solution)/shard_map/ppermute | solution.py:681
  386.9 47.4 %collective-permute-start.34 = (bf16[4,144,768]{2,1,0:T(8,128)(2,1)}, bf16[4,144,768]{2,1,0:T(8,128)(2,1)}, u32[]{:S(2)}, u32[]{:S(2)}) collective-permute-start(bf16[4,144,768]{2,1,0:T(8,128)(2,1)} %pad_maximum_fusion.3), channel_id=1, source_target_pairs={{0,4},{1,5},{2,6},{3,7},{4,0},{5,1},{6,2},{7,3},{8,12},{9,13},{10,... | collective-permute-start | bytes 2654216 | tf_op jit(solution)/shard_map/ppermute | solution.py:681
  415.1 9.8 %copy-start.27 = (bf16[96,768]{1,0:T(8,128)(2,1)S(1)}, bf16[96,768]{1,0:T(8,128)(2,1)}, u32[]{:S(2)}) copy-start(bf16[96,768]{1,0:T(8,128)(2,1)} %copy-done.26) | copy-start | bytes 442372
  415.1 17.8 %copy-start.12 = (bf16[2,112,768]{2,1,0:T(8,128)(2,1)S(1)}, bf16[2,112,768]{2,1,0:T(8,128)(2,1)}, u32[]{:S(2)}) copy-start(bf16[2,112,768]{2,1,0:T(8,128)(2,1)} %copy-done.11) | copy-start | bytes 1032196
  415.1 17.8 %copy-start.18 = (bf16[1,112,768]{2,1,0:T(8,128)(2,1)S(1)}, bf16[1,112,768]{2,1,0:T(8,128)(2,1)}, u32[]{:S(2)}) copy-start(bf16[1,112,768]{2,1,0:T(8,128)(2,1)} %copy-done.16) | copy-start | bytes 516100
  424.9 7.0 %collective-permute-start.37 = (bf16[2,48,768]{2,1,0:T(8,128)(2,1)S(1)}, bf16[2,48,768]{2,1,0:T(8,128)(2,1)S(1)}, u32[]{:S(2)}, u32[]{:S(2)}) collective-permute-start(bf16[2,48,768]{2,1,0:T(8,128)(2,1)S(1)} %pad_maximum_fusion.14), channel_id=1, source_target_pairs={{0,8},{1,9},{2,10},{3,11},{4,12},{5,13},{6,14},{7,15},{8,0},{9,1},... | collective-permute-start | bytes 442376 | tf_op jit(solution)/shard_map/ppermute | solution.py:681
  425.0 9.3 %copy-start.3 = (bf16[2,144,768]{2,1,0:T(8,128)(2,1)S(1)}, bf16[2,144,768]{2,1,0:T(8,128)(2,1)}, u32[]{:S(2)}) copy-start(bf16[2,144,768]{2,1,0:T(8,128)(2,1)} %copy-done.2) | copy-start | bytes 1327108
  425.0 9.3 %copy-start.5 = (bf16[1,144,768]{2,1,0:T(8,128)(2,1)S(1)}, bf16[1,144,768]{2,1,0:T(8,128)(2,1)}, u32[]{:S(2)}) copy-start(bf16[1,144,768]{2,1,0:T(8,128)(2,1)} %copy-done.4) | copy-start | bytes 663556
  425.0 9.3 %copy-start.8 = (bf16[1,144,768]{2,1,0:T(8,128)(2,1)S(1)}, bf16[1,144,768]{2,1,0:T(8,128)(2,1)}, u32[]{:S(2)}) copy-start(bf16[1,144,768]{2,1,0:T(8,128)(2,1)} %copy-done.6) | copy-start | bytes 663556
  432.9 6.8 %collective-permute-start.38 = (bf16[4,48,768]{2,1,0:T(8,128)(2,1)S(1)}, bf16[4,48,768]{2,1,0:T(8,128)(2,1)S(1)}, u32[]{:S(2)}, u32[]{:S(2)}) collective-permute-start(bf16[4,48,768]{2,1,0:T(8,128)(2,1)S(1)} %pad_maximum_fusion.13), channel_id=1, source_target_pairs={{0,4},{1,5},{2,6},{3,7},{4,0},{5,1},{6,2},{7,3},{8,12},{9,13},{10,... | collective-permute-start | bytes 884744 | tf_op jit(solution)/shard_map/ppermute | solution.py:681
  434.2 6.5 %copy-start.24 = (bf16[16,48,768]{2,1,0:T(8,128)(2,1)S(1)}, bf16[16,48,768]{2,1,0:T(8,128)(2,1)}, u32[]{:S(2)}) copy-start(bf16[16,48,768]{2,1,0:T(8,128)(2,1)} %constant_dynamic-update-slice_fusion.8) | copy-start | bytes 3538948
  434.2 11.3 %collective-permute-start.43 = (bf16[8,112,768]{2,1,0:T(8,128)(2,1)S(1)}, bf16[8,112,768]{2,1,0:T(8,128)(2,1)S(1)}, u32[]{:S(2)}, u32[]{:S(2)}) collective-permute-start(bf16[8,112,768]{2,1,0:T(8,128)(2,1)S(1)} %pad_maximum_fusion.2), channel_id=1, source_target_pairs={{0,1},{1,0},{2,3},{3,2},{4,5},{5,4},{6,7},{7,6},{8,9},{9,8},{10,11... | collective-permute-start | bytes 4128776 | tf_op jit(solution)/shard_map/ppermute | solution.py:681
  437.1 24.9 %collective-permute-start.35 = (bf16[8,144,768]{2,1,0:T(8,128)(2,1)}, bf16[8,144,768]{2,1,0:T(8,128)(2,1)}, u32[]{:S(2)}, u32[]{:S(2)}) collective-permute-start(bf16[8,144,768]{2,1,0:T(8,128)(2,1)} %pad_maximum_fusion.1), channel_id=1, source_target_pairs={{0,1},{1,0},{2,3},{3,2},{4,5},{5,4},{6,7},{7,6},{8,9},{9,8},{10,11... | collective-permute-start | bytes 5308424 | tf_op jit(solution)/shard_map/ppermute | solution.py:681
  440.6 2.1 collective-permute-start.39
  (22 other events, 62.4 us)
